TPU v7x, 512 devices: a whole 4x8x8 slice. The times are simulated.
512 devices in a mesh: gy: 32 (over y, x), gz: 16 (over z, core).
Axes of the slice: x: 4, y: 8, z: 8, core: 2. Of those that a mesh axis runs over, the one named last changes fastest.
Arguments:
- rhs: float32 [5, 4, 64, 32, 128], P(None, None, 'gy', 'gz'), may hold values from -6 to 6
- bc_codes: int32 [4, 64, 32, 128], P(None, 'gy', 'gz'), may hold values from 0 to 2
- line_pivots: float32 [5, 5, 4, 64, 32, 128], P(None, None, None, 'gy', 'gz'), may hold values from -0.6 to 1.4
- x_lower: float32 [5, 5, 3, 64, 32, 128], P(None, None, None, 'gy', 'gz'), may hold values from -0.9 to 0.9
- x_upper: float32 [5, 5, 3, 64, 32, 128], P(None, None, None, 'gy', 'gz'), may hold values from -0.9 to 0.9
- lower_coupling: float32 [2, 5, 5, 4, 64, 32, 128], P(None, None, None, None, 'gy', 'gz'), may hold values from -0.54 to 0.15
- upper_coupling: float32 [2, 5, 5, 4, 64, 32, 128], P(None, None, None, None, 'gy', 'gz'), may hold values from -0.54 to 0.15
- cell_volume: float32 [64, 32], P('gy', 'gz'), may hold values from 0.05 to 0.5
Outputs:
- correction: float32 [5, 4, 64, 32, 128], P(None, None, 'gy', 'gz')
- coarse_residual: float32 [5, 4, 64, 128], P(None, None, 'gy', 'gz')
All inputs are finite; a program needn't handle non-finite values.
Results may differ from a plain program's by a relative error of at most 0.00012.
Values sent between devices are 32-bit elements; how exact they have to be, the bound alone decides.
No kernel may reach another device: no remote copies, remote signals or barrier semaphores. Data moves between devices by JAX's collectives and lax.ppermute only.
A program may use at most 64 MiB of HBM per device.

v0:
```python
import jax
import jax.numpy as jnp
from jax import lax
from jax.sharding import PartitionSpec as P

PLANES = 4
ITERS = 2


def from_behind(x, axis, by):
    size = lax.axis_size(axis)
    pairs = [(i, i + by) for i in range(size) if 0 <= i + by < size]
    return lax.ppermute(x, axis, pairs)


def apply_block(matrix, vector):
    return jnp.sum(matrix * vector[None], axis=1)


def line_solve(pivots, x_lower, x_upper, source):
    forward_values = []
    for plane in range(PLANES):
        current = source[:, plane]
        if plane > 0:
            current = current - apply_block(x_lower[:, :, plane - 1], forward_values[plane - 1])
        forward_values.append(apply_block(pivots[:, :, plane], current))
    solved = [None] * PLANES
    solved[PLANES - 1] = forward_values[PLANES - 1]
    for plane in range(PLANES - 2, -1, -1):
        solved[plane] = forward_values[plane] - apply_block(
            pivots[:, :, plane], apply_block(x_upper[:, :, plane], solved[plane + 1])
        )
    return jnp.stack(solved, axis=1)


def masked_source(rhs, bc_codes):
    component = lax.broadcasted_iota(jnp.int32, (5, 1, 1, 1, 1), 0)
    wall = (bc_codes == 1)[None]
    symmetry = (bc_codes == 2)[None]
    removed = wall & (component >= 1) & (component <= 3) | symmetry & (component == 3)
    return jnp.where(removed, jnp.zeros_like(rhs), rhs)


def neighbor_terms(values_in, coupling, offset):
    if offset == 1:
        edge_y = values_in[:, :, -1]
        edge_z = values_in[:, :, :, -1]
    else:
        edge_y = values_in[:, :, 0]
        edge_z = values_in[:, :, :, 0]
    got_y = from_behind(edge_y, "gy", offset)
    got_z = from_behind(edge_z, "gz", offset)
    if offset == 1:
        along_y = jnp.concatenate([got_y[:, :, None], values_in[:, :, :-1]], axis=2)
        along_z = jnp.concatenate([got_z[:, :, :, None], values_in[:, :, :, :-1]], axis=3)
    else:
        along_y = jnp.concatenate([values_in[:, :, 1:], got_y[:, :, None]], axis=2)
        along_z = jnp.concatenate([values_in[:, :, :, 1:], got_z[:, :, :, None]], axis=3)
    return apply_block(coupling[0], along_y) + apply_block(coupling[1], along_z)


def local_sweep(source_terms, couple_y, couple_z, pivots, x_lower, x_upper, incoming_y, incoming_z):
    cells_y = source_terms.shape[2]
    cells_z = source_terms.shape[3]
    done_rows = []
    for j in range(cells_y):
        row_cells = []
        for k in range(cells_z):
            above_value = incoming_y[:, :, k] if j == 0 else done_rows[j - 1][k]
            left_value = incoming_z[:, :, j] if k == 0 else row_cells[k - 1]
            current = (
                source_terms[:, :, j, k]
                - apply_block(couple_y[:, :, :, j, k], above_value)
                - apply_block(couple_z[:, :, :, j, k], left_value)
            )
            row_cells.append(
                line_solve(
                    pivots[:, :, :, j, k], x_lower[:, :, :, j, k], x_upper[:, :, :, j, k], current
                )
            )
        done_rows.append(row_cells)
    return jnp.stack([jnp.stack(row_cells, axis=2) for row_cells in done_rows], axis=2)


def wavefront(
    source_terms, couple_y, couple_z, pivots, x_lower, x_upper, rank, last_rank, groups, offset
):
    cells_y = source_terms.shape[2]
    cells_z = source_terms.shape[3]
    slabs = source_terms.shape[4]
    group_width = slabs // groups

    def advance(step_now, state_now):
        local_block, face_y, face_z = state_now
        incoming_y = from_behind(face_y, "gy", offset)
        incoming_z = from_behind(face_z, "gz", offset)
        group_now = step_now - rank
        active = (group_now >= 0) & (group_now < groups)
        start_at = jnp.clip(group_now, 0, groups - 1) * group_width

        def compute(operand):
            fresh = local_sweep(
                source_terms, couple_y, couple_z, pivots, x_lower, x_upper, incoming_y, incoming_z
            )
            updated = lax.dynamic_update_slice_in_dim(local_block, fresh, start_at, 4)
            return (updated, fresh[:, :, -1], fresh[:, :, :, -1])

        def unchanged(operand):
            return (local_block, face_y, face_z)

        return lax.cond(active, compute, unchanged, 0)

    start_state = (
        jnp.zeros_like(source_terms),
        jnp.zeros((5, PLANES, cells_z, group_width), jnp.float32),
        jnp.zeros((5, PLANES, cells_y, group_width), jnp.float32),
    )
    final_state = lax.fori_loop(0, last_rank + groups, advance, start_state)
    return final_state[0]


def flipped(array_in):
    return jnp.flip(array_in, axis=(array_in.ndim - 3, array_in.ndim - 2))


def on_device(
    rhs, bc_codes, line_pivots, x_lower, x_upper, lower_coupling, upper_coupling, cell_volume
):
    source = masked_source(rhs, bc_codes)
    groups = 1
    index_y = lax.axis_index("gy")
    index_z = lax.axis_index("gz")
    count_y = lax.axis_size("gy")
    count_z = lax.axis_size("gz")
    forward_rank = index_y + index_z
    backward_rank = count_y - 1 - index_y + (count_z - 1 - index_z)
    last_rank = count_y + count_z - 2
    back_couple_y = flipped(upper_coupling[0])
    back_couple_z = flipped(upper_coupling[1])
    back_pivots = flipped(line_pivots)
    back_lower = flipped(x_lower)
    back_upper = flipped(x_upper)
    correction = jnp.zeros_like(source)
    forward_pass = source
    for iteration in range(ITERS):
        if iteration == 0:
            forward_source = source
        else:
            forward_source = source - neighbor_terms(correction, upper_coupling, -1)
        forward_pass = wavefront(
            forward_source,
            lower_coupling[0],
            lower_coupling[1],
            line_pivots,
            x_lower,
            x_upper,
            forward_rank,
            last_rank,
            groups,
            1,
        )
        backward_source = source - neighbor_terms(forward_pass, lower_coupling, 1)
        backward_pass = wavefront(
            flipped(backward_source),
            back_couple_y,
            back_couple_z,
            back_pivots,
            back_lower,
            back_upper,
            backward_rank,
            last_rank,
            groups,
            -1,
        )
        correction = flipped(backward_pass)
    residual = neighbor_terms(forward_pass - correction, lower_coupling, 1)
    partial_sums = jnp.sum(cell_volume[None, None, :, :, None] * residual, axis=3)
    coarse_residual = lax.psum_scatter(partial_sums, "gz", scatter_dimension=3, tiled=True)
    return (correction, coarse_residual)


def solution(mesh):
    return jax.shard_map(
        on_device,
        mesh=mesh,
        in_specs=(
            P(None, None, "gy", "gz", None),
            P(None, "gy", "gz", None),
            P(None, None, None, "gy", "gz", None),
            P(None, None, None, "gy", "gz", None),
            P(None, None, None, "gy", "gz", None),
            P(None, None, None, None, "gy", "gz", None),
            P(None, None, None, None, "gy", "gz", None),
            P("gy", "gz"),
        ),
        out_specs=(P(None, None, "gy", "gz", None), P(None, None, "gy", "gz")),
        check_vma=False,
    )
```

profile of v0, /device:TPU:1, one launch (start us, length us, event | category | flops | bytes accessed | tf_op | source)
XLA Modules:
  0.0 1820.5 jit_solution(621812690338830555)
XLA Ops:
  4.6 433.2 %while.68 = (s32[]{:T(128)}, f32[5,4,2,2,128]{4,1,0,3,2:T(4,128)S(1)}, f32[5,4,2,128]{3,1,0,2:T(4,128)S(1)}, f32[5,4,2,128]{3,1,0,2:T(4,128)S(1)}, s32[]{:T(128)...) while((s32[]{:T(128)}, ...), condition=%wide.region_63.64_spmd, body=%wide.region_0.63_spmd.sunk | while | flops 581127 | bytes 5325163 | solution.py:118
  31.1 6.3 collective-permute-start
  42.7 7.6 collective-permute-start.1
  121.1 7.4 collective-permute-start.1
  136.7 6.4 collective-permute-start
  151.0 7.6 collective-permute-start.1
  179.8 6.9 collective-permute-start.1
  208.0 7.3 collective-permute-start.1
  218.2 5.7 collective-permute-start.1
  228.8 5.7 collective-permute-start.1
  247.3 5.7 collective-permute-start.1
  255.8 5.7 collective-permute-start.1
  274.3 5.7 collective-permute-start.1
  284.9 5.7 collective-permute-start.1
  293.4 5.7 collective-permute-start.1
  304.1 5.7 collective-permute-start.1
  312.6 5.7 collective-permute-start.1
  440.2 5.7 collective-permute-start.9
  450.9 427.7 %while.69 = (s32[]{:T(128)}, f32[5,4,2,2,128]{4,1,0,3,2:T(4,128)S(1)}, f32[5,4,2,128]{3,1,0,2:T(4,128)S(1)}, f32[5,4,2,128]{3,1,0,2:T(4,128)S(1)}, s32[]{:T(128)...) while((s32[]{:T(128)}, ...), condition=%wide.region_129.130_spmd, body=%wide.region_66.129_spmd.sunk | while | flops 581127 | bytes 5325163 | solution.py:118
  823.1 45.7 %collective-permute-done.2 = f32[5,4,2,128]{3,1,0,2:T(4,128)S(1)} collective-permute-done((f32[5,4,2,128]{3,1,0,2:T(4,128)S(1)}, f32[5,4,2,128]{3,1,0,2:T(4,128)S(1)}, u32[]{:S(2)}, u32[]{:S(2)}) %collective-permute-start.2) | collective-permute-done | bytes 20512 | tf_op jit(solution)/shard_map/while/body/eval_jaxpr/ppermute | solution.py:13
  885.3 444.8 %while.70 = (s32[]{:T(128)}, f32[5,4,2,2,128]{4,1,0,3,2:T(4,128)S(1)}, f32[5,4,2,128]{3,1,0,2:T(4,128)S(1)}, f32[5,4,2,128]{3,1,0,2:T(4,128)S(1)}, s32[]{:T(128)...) while((s32[]{:T(128)}, ...), condition=%wide.region_195.196_spmd, body=%wide.region_132.195_spmd.sunk | while | flops 581127 | bytes 5325163 | solution.py:118
  910.4 7.8 collective-permute-start.4
  923.2 7.4 collective-permute-start.5
  991.1 8.3 collective-permute-start.4
  1009.2 6.3 collective-permute-start.5
  1016.3 7.7 collective-permute-start.4
  1041.7 6.3 collective-permute-start.5
  1069.5 8.1 collective-permute-start.5
  1098.2 7.1 collective-permute-start.5
  1339.2 428.6 %while.71 = (s32[]{:T(128)}, f32[5,4,2,2,128]{4,1,0,3,2:T(4,128)S(1)}, f32[5,4,2,128]{3,1,0,2:T(4,128)S(1)}, f32[5,4,2,128]{3,1,0,2:T(4,128)S(1)}, s32[]{:T(128)...) while((s32[]{:T(128)}, ...), condition=%wide.region_261.262_spmd, body=%wide.region_198.261_spmd.sunk | while | flops 581127 | bytes 5325163 | solution.py:118
  1711.7 46.4 %collective-permute-done.6 = f32[5,4,2,128]{3,1,0,2:T(4,128)S(1)} collective-permute-done((f32[5,4,2,128]{3,1,0,2:T(4,128)S(1)}, f32[5,4,2,128]{3,1,0,2:T(4,128)S(1)}, u32[]{:S(2)}, u32[]{:S(2)}) %collective-permute-start.6) | collective-permute-done | bytes 20512 | tf_op jit(solution)/shard_map/while/body/eval_jaxpr/ppermute | solution.py:13
  1776.3 43.5 %all-reduce = f32[5,4,2,128]{3,2,1,0:T(2,128)S(1)} all-reduce(f32[5,4,2,128]{3,2,1,0:T(2,128)S(1)} %copy.100), channel_id=2, replica_groups=mesh['gy'=32,'gz'=16] {'gz'}, use_global_device_ids=true, to_apply=%region_265.266.clone | all-reduce | flops 5120 | bytes 40960
  (1581 shorter events, 1520.2 us)
Async XLA Ops:
  40.6 9.7 collective-permute-start
  91.9 10.1 collective-permute-start
  118.7 9.8 collective-permute-start
  136.7 10.9 collective-permute-start
  148.6 10.0 collective-permute-start
  166.8 10.0 collective-permute-start
  195.6 9.1 collective-permute-start
  205.6 9.7 collective-permute-start
  224.8 9.8 collective-permute-start
  280.9 9.7 collective-permute-start
  300.0 9.8 collective-permute-start
  372.0 11.0 collective-permute-start
  437.8 11.9 collective-permute-start.8
  440.2 9.6 collective-permute-start.9
  819.9 48.9 %collective-permute-start.2 = (f32[5,4,2,128]{3,1,0,2:T(4,128)S(1)}, f32[5,4,2,128]{3,1,0,2:T(4,128)S(1)}, u32[]{:S(2)}, u32[]{:S(2)}) collective-permute-start(f32[5,4,2,128]{3,1,0,2:T(4,128)S(1)} %get-tuple-element.1894), channel_id=1, source_target_pairs={{16,0},{32,16},{48,32},{64,48},{80,64},{96,80},{112,96},{128,112},... | collective-permute-start | bytes 61448 | tf_op jit(solution)/shard_map/while/body/eval_jaxpr/ppermute | solution.py:13
  821.1 47.9 %collective-permute-start.3 = (f32[5,4,2,128]{3,1,0,2:T(4,128)S(1)}, f32[5,4,2,128]{3,1,0,2:T(4,128)S(1)}, u32[]{:S(2)}, u32[]{:S(2)}) collective-permute-start(f32[5,4,2,128]{3,1,0,2:T(4,128)S(1)} %get-tuple-element.1895), channel_id=1, source_target_pairs={{1,0},{2,1},{3,2},{4,3},{5,4},{6,5},{7,6},{8,7},{9,8},{10,9},{11,1... | collective-permute-start | bytes 61448 | tf_op jit(solution)/shard_map/while/body/eval_jaxpr/ppermute | solution.py:13
  910.4 9.8 collective-permute-start.4
  921.3 9.3 collective-permute-start.4
  954.9 9.6 collective-permute-start.4
  972.3 10.1 collective-permute-start.4
  991.1 12.8 collective-permute-start.4
  1004.8 10.7 collective-permute-start.4
  1016.3 12.3 collective-permute-start.4
  1038.5 9.5 collective-permute-start.4
  1066.6 11.1 collective-permute-start.4
  1085.8 9.5 collective-permute-start.4
  1115.0 10.7 collective-permute-start.4
  1153.5 11.1 collective-permute-start.4
  1192.4 9.8 collective-permute-start.4
  1264.3 11.0 collective-permute-start.4
  1708.4 49.6 %collective-permute-start.6 = (f32[5,4,2,128]{3,1,0,2:T(4,128)S(1)}, f32[5,4,2,128]{3,1,0,2:T(4,128)S(1)}, u32[]{:S(2)}, u32[]{:S(2)}) collective-permute-start(f32[5,4,2,128]{3,1,0,2:T(4,128)S(1)} %get-tuple-element.1972), channel_id=1, source_target_pairs={{16,0},{32,16},{48,32},{64,48},{80,64},{96,80},{112,96},{128,112},... | collective-permute-start | bytes 61448 | tf_op jit(solution)/shard_map/while/body/eval_jaxpr/ppermute | solution.py:13
  1709.7 48.6 %collective-permute-start.7 = (f32[5,4,2,128]{3,1,0,2:T(4,128)S(1)}, f32[5,4,2,128]{3,1,0,2:T(4,128)S(1)}, u32[]{:S(2)}, u32[]{:S(2)}) collective-permute-start(f32[5,4,2,128]{3,1,0,2:T(4,128)S(1)} %get-tuple-element.1973), channel_id=1, source_target_pairs={{1,0},{2,1},{3,2},{4,3},{5,4},{6,5},{7,6},{8,7},{9,8},{10,9},{11,1... | collective-permute-start | bytes 61448 | tf_op jit(solution)/shard_map/while/body/eval_jaxpr/ppermute | solution.py:13
  (359 other events, 2923.8 us)
where the time goes:
time: 1850 us; the launch traced here: 1820 us
  starting transfers between devices  1110 us (60%)
  waiting for transfers between devices  631 us (34%)
  blocking collectives  43.5 us (2%)
    ppermute x384, starting transfers between devices, from_behind(): return lax.ppermute(x, axis, pairs)  1110 us
    ppermute x384, waiting for transfers between devices, from_behind(): return lax.ppermute(x, axis, pairs)  631 us
    unnamed x1, blocking collectives  43.5 us
  transfers between devices with their start and end apart: 384, of which 285 were waited for; matrix products, arithmetic and copies ran while one was open for 0% of the time, Pallas kernels for 0%

commit v1 on v0

v1 whole, which is shorter than its diff:
```python
import jax
import jax.numpy as jnp
from jax import lax
from jax.experimental import pallas as pl
from jax.experimental.pallas import tpu as pltpu
from jax.sharding import Mesh, PartitionSpec as P

F32 = jnp.float32
NZ = 32
NY = 64
DIAGS = NY + NZ - 1
PITCH = 272
SWAP = [(0, 1), (1, 0)]
GROUP = ("z", "cy", "xh")
SMEM = pltpu.SMEM
VMEM = pltpu.VMEM


def tree(terms):
    terms = list(terms)
    while len(terms) > 1:
        terms = [
            terms[k] + terms[k + 1] if k + 1 < len(terms) else terms[k]
            for k in range(0, len(terms), 2)
        ]
    return terms[0]


def spread(value, i):
    return jnp.broadcast_to(value[i : i + 1, :], (8, 128))


def pack_kernel(meta, vol, rhs, codes, piv, low_x, up_x, low, up, out, tile):
    first_z = meta[2]
    last_z = meta[3]
    zero = jnp.zeros((25, 128), F32)
    component = lax.broadcasted_iota(jnp.int32, (5, 128), 0)
    for jz in range(2):
        for jy in range(2):
            for p in range(4):
                at = p * 4 + jy * 2 + jz
                t = tile.at[(jy * 4 + p) % 2]
                t[0:25, :] = piv[pl.ds(at, 25, stride=16), :]
                t[25:50, :] = low_x[pl.ds(at - 4, 25, stride=12), :] if p > 0 else zero
                t[50:75, :] = up_x[pl.ds(at, 25, stride=12), :] if p < 3 else zero
                t[75:100, :] = low[pl.ds(at, 25, stride=16), :]
                along_z = low[pl.ds(400 + at, 25, stride=16), :]
                if jz == 0:
                    along_z = jnp.where(first_z == 1, 0.0, along_z)
                t[100:125, :] = along_z
                t[125:128, :] = zero[:3]
                out[pl.ds(jz * 8 + jy * 4 + p, 128, stride=24), :] = t[...].T
    for jz in range(2):
        for p in range(4):
            t = tile.at[p % 2]
            for jy in range(2):
                at = p * 4 + jy * 2 + jz
                base = 64 * jy
                t[base : base + 25, :] = up[pl.ds(at, 25, stride=16), :]
                along_z = up[pl.ds(400 + at, 25, stride=16), :]
                if jz == 1:
                    along_z = jnp.where(last_z == 1, 0.0, along_z)
                t[base + 25 : base + 50, :] = along_z
                code = jnp.broadcast_to(codes[at : at + 1, :], (5, 128))
                removed = ((code == 1) & (component >= 1) & (component <= 3)) | (
                    (code == 2) & (component == 3)
                )
                t[base + 50 : base + 55, :] = jnp.where(
                    removed, 0.0, rhs[pl.ds(at, 5, stride=16), :]
                )
                t[base + 55 : base + 64, :] = jnp.full((9, 128), vol[jy, jz], F32)
            out[pl.ds(16 + jz * 4 + p, 128, stride=24), :] = t[...].T


def column(ref, d, base, j):
    return ref[d, pl.ds(base + j, 8, stride=5), :]


def row(ref, d, r):
    return jnp.broadcast_to(ref[d, pl.ds(r, 1), :], (8, 128))


def main_kernel(
    meta, q0, q1, q2, q3, out, df, du, tf, tu, tmp, al, au, g, vv, f1, c1, rl, ru, sem
):
    core = meta[0]
    side = meta[1]
    copies = []
    for n, (q, dc, dx) in enumerate(((q0, 0, 0), (q1, 1, 0), (q2, 0, 1), (q3, 1, 1))):
        c = core + dc - 2 * core * dc
        x = side + dx - 2 * side * dx
        for part in range(3):
            src = q.at[:, :, pl.ds(8 * part, 8), :]
            dst = (
                df.at[:, c, part, pl.ds(0, 16), x] if part < 2 else du.at[:, c, pl.ds(0, 16), x]
            )
            copies.append(pltpu.make_async_copy(src, dst, sem.at[n * 3 + part]))
    for copy in copies:
        copy.start()
    for copy in copies:
        copy.wait()
    fl = df.reshape(32 * PITCH, 128)
    ul = du.reshape(16 * PITCH, 128)
    lane = lax.broadcasted_iota(jnp.int32, (8, 128), 1)
    sub = lax.broadcasted_iota(jnp.int32, (8, 128), 0)
    z = lane & 31
    even_z = (lane & 1) == 0

    def turn_f(d, carry):
        block = jnp.concatenate(
            [fl[pl.ds(4 * d + p, 32, stride=PITCH - 4), :] for p in range(4)], axis=0
        )
        tf[d, pl.ds(0, 128), :] = block.T
        return carry

    lax.fori_loop(0, DIAGS, turn_f, 0, unroll=5)

    def turn_u(e, carry):
        for p in range(4):
            for jz in range(2):
                tmp[pl.ds(p * 32 + jz, 16, stride=2), :] = ul[
                    pl.ds(8 * e + jz * 4 + p, 16, stride=PITCH - 8), :
                ]
        tu[pl.ds(pl.multiple_of(128 * e + 128, 128), 128), :] = tmp[...].T
        return carry

    lax.fori_loop(0, 47, turn_u, 0)

    def prepare(d, carry):
        piv = [column(tf, d, 0, i) for i in range(5)]
        pl_cols = [tree([piv[i] * row(tf, d, 25 + 5 * i + j) for i in range(5)]) for j in range(5)]
        pu_cols = [tree([piv[i] * row(tf, d, 50 + 5 * i + j) for i in range(5)]) for j in range(5)]

        def times(left, right):
            return [tree([left[i] * spread(right[j], i) for i in range(5)]) for j in range(5)]

        def shifted(cols, by):
            return [pltpu.roll(v, by, 1) for v in cols]

        w = [piv]
        for _ in range(3):
            w.append([-v for v in times(pl_cols, shifted(w[-1], 32))])
        inverse = {3: w[3]}
        for s in (2, 1, 0, -1, -2, -3):
            below = times(pu_cols, shifted(inverse[s + 1], 96))
            inverse[s] = [w[s][j] - below[j] if s >= 0 else -below[j] for j in range(5)]
        full = [inverse[0]] + [
            [a + b for a, b in zip(inverse[s], inverse[s - 4])] for s in (1, 2, 3)
        ]
        for k in range(7):
            v = tf[d, pl.ds(72 + 8 * k, 8), :]
            for s in range(4):
                rl[s, pl.ds(8 * k, 8), :] = v if s == 0 else pltpu.roll(v, 32 * s, 1)
        for k in range(8):
            even = tu[pl.ds(pl.multiple_of(64 * d + 128, 64) + 8 * k, 8), :]
            odd = tu[pl.ds(pl.multiple_of(64 * d + 64, 64) + 8 * k, 8), :]
            v = jnp.where(even_z, even, odd)
            for s in range(4):
                ru[s, pl.ds(8 * k, 8), :] = v if s == 0 else pltpu.roll(v, 32 * s, 1)
        for s in range(4):
            for n, (dest, source, base) in enumerate(
                ((al, rl, 3), (al, rl, 28), (au, ru, 0), (au, ru, 25))
            ):
                for j in range(5):
                    dest[d, pl.ds(8 * (s * 10 + 5 * (n % 2) + j), 8), :] = tree(
                        [full[s][i] * row(source, s, base + 5 * i + j) for i in range(5)]
                    )
        g[d] = tree([full[s][i] * row(ru, s, 50 + i) for s in range(4) for i in range(5)])
        vv[d] = row(ru, 0, 55)
        return carry

    lax.fori_loop(0, DIAGS, prepare, 0)

    def product(ref, d, f, step):
        terms = []
        for s in range(4):
            by_y = f if s == 0 else pltpu.roll(f, 32 * s, 1)
            by_z = pltpu.roll(f, (32 * s + step) % 128, 1)
            for i in range(5):
                terms.append(ref[d, pl.ds(8 * (s * 10 + i), 8), :] * spread(by_y, i))
            for i in range(5):
                terms.append(ref[d, pl.ds(8 * (s * 10 + 5 + i), 8), :] * spread(by_z, i))
        return tree(terms)

    def inside(d):
        return (z <= d) & (z >= d - (NY - 1))

    nothing = jnp.zeros((8, 128), F32)

    def forward_first(d, f):
        f = jnp.where(inside(d), g[d] - product(al, d, f, 1), 0.0)
        f1[d] = f
        return f

    lax.fori_loop(0, DIAGS, forward_first, nothing)

    def backward_first(n, f):
        d = DIAGS - 1 - n
        coupled = product(au, d, f, -1)
        f = jnp.where(inside(d), f1[d] - coupled, 0.0)
        f1[d] = f
        g[d] = coupled
        return f

    lax.fori_loop(0, DIAGS, backward_first, nothing)

    def forward_second(d, f):
        coupled = product(al, d, f, 1)
        f = jnp.where(inside(d), -(g[d] + coupled), 0.0)
        c1[d] = coupled
        return f

    lax.fori_loop(0, DIAGS, forward_second, nothing)

    def backward_second(n, f):
        d = DIAGS - 1 - n
        coupled = product(au, d, f, -1)
        f = jnp.where(inside(d), -(c1[d] + coupled), 0.0)
        f1[d] = f1[d] + f
        c1[d] = jnp.where(inside(d), coupled, 0.0)
        return f

    lax.fori_loop(0, DIAGS, backward_second, nothing)

    def residual(d, before):
        by_z = pltpu.roll(before, 1, 1)
        g[d] = vv[d] * tree(
            [column(tf, d, 75, i) * spread(before, i) for i in range(5)]
            + [column(tf, d, 100, i) * spread(by_z, i) for i in range(5)]
        )
        return c1[d]

    lax.fori_loop(0, DIAGS, residual, nothing)
    for bit, length in ((16, 79), (8, 71), (4, 67), (2, 65), (1, 64)):

        def straighten(d, carry, bit=bit):
            far = (z & bit) != 0
            f1[d] = jnp.where(far, f1[d + bit], f1[d])
            g[d] = jnp.where(far, g[d + bit], g[d])
            return carry

        lax.fori_loop(0, length, straighten, 0)

    owner_y = lane & 15
    owner_z = lane >> 4

    def collect(n, sums):
        sums = list(sums)
        for jy in range(2):
            y = 4 * n + 2 * side + jy
            value = f1[y]
            total = g[y]
            for by in (16, 8, 4, 2, 1):
                total = total + pltpu.roll(total, 128 - by, 1)
            for jz in range(2):
                merged = jnp.where(sub < 5, value, pltpu.roll(total, 5 if jz == 0 else 2, 0))
                for p in range(4):
                    index = jnp.where(sub < 5, p * 32 + 4 * owner_z + 2 * core + jz, p * 32)
                    picked = jnp.take_along_axis(merged, index, axis=1)
                    k = p * 4 + jz * 2 + jy
                    sums[k] = jnp.where(owner_y == n, picked, sums[k])
        return tuple(sums)

    slots = lax.fori_loop(0, 16, collect, (nothing,) * 16)
    out[...] = jnp.concatenate(slots, axis=0).T


def unpack_kernel(meta, slots, correction, coarse):
    values = slots[...].T
    gz = meta[4]
    for p in range(4):
        for jy in range(2):
            for jz in range(2):
                k = 8 * (p * 4 + jz * 2 + jy)
                correction[pl.ds(p * 4 + jy * 2 + jz, 5, stride=16), :] = values[k : k + 5]
                extra = pltpu.roll(values[k : k + 8], (128 - 8 * gz) % 128, 1)
                if jz == 0:
                    coarse[pl.ds(p * 2 + jy, 3, stride=8), :] = extra[5:8]
                else:
                    coarse[pl.ds(24 + p * 2 + jy, 2, stride=8), :] = extra[5:7]


def on_device(rhs, codes, piv, low_x, up_x, low, up, volume):
    core = lax.axis_index("c")
    side = lax.axis_index("xl")
    gz = lax.axis_index("z") * 2 + core
    meta = jnp.stack(
        [core, side, (gz == 0).astype(jnp.int32), (gz == 15).astype(jnp.int32), gz]
    ).astype(jnp.int32)
    smem = pl.BlockSpec(memory_space=SMEM)
    vmem = pl.BlockSpec(memory_space=VMEM)
    hbm = pl.BlockSpec(memory_space=pl.ANY)
    packed = pl.pallas_call(
        pack_kernel,
        out_shape=jax.ShapeDtypeStruct((128 * 24, 128), F32),
        in_specs=[smem, smem] + [vmem] * 7,
        out_specs=vmem,
        scratch_shapes=[pltpu.VMEM((2, 128, 128), F32)],
        compiler_params=pltpu.CompilerParams(vmem_limit_bytes=32 << 20),
        name="pack",
    )(
        meta,
        volume,
        rhs.reshape(80, 128),
        codes.reshape(16, 128),
        piv.reshape(400, 128),
        low_x.reshape(300, 128),
        up_x.reshape(300, 128),
        low.reshape(800, 128),
        up.reshape(800, 128),
    )
    mine = lax.all_to_all(packed.reshape(128, 24, 128), GROUP, 0, 0, tiled=True)
    other_x = lax.ppermute(mine, "xl", SWAP)
    other_c = lax.ppermute(mine, "c", SWAP)
    other_cx = lax.ppermute(other_x, "c", SWAP)
    quarters = [v.reshape(8, 16, 24, 128) for v in (mine, other_c, other_x, other_cx)]
    diag = pltpu.VMEM((96, 8, 128), F32)
    slots = pl.pallas_call(
        main_kernel,
        out_shape=jax.ShapeDtypeStruct((128, 128), F32),
        in_specs=[smem] + [hbm] * 4,
        out_specs=vmem,
        scratch_shapes=[
            pltpu.VMEM((8, 2, 2, 17, 2, 8, 128), F32),
            pltpu.VMEM((8, 2, 17, 2, 8, 128), F32),
            pltpu.VMEM((DIAGS, 144, 128), F32),
            pltpu.VMEM((50 * 128, 128), F32),
            pltpu.VMEM((128, 128), F32),
            pltpu.VMEM((DIAGS, 320, 128), F32),
            pltpu.VMEM((DIAGS, 320, 128), F32),
            diag,
            diag,
            diag,
            diag,
            pltpu.VMEM((4, 56, 128), F32),
            pltpu.VMEM((4, 64, 128), F32),
            pltpu.SemaphoreType.DMA((12,)),
        ],
        compiler_params=pltpu.CompilerParams(vmem_limit_bytes=60 << 20),
        name="sweeps",
    )(meta, *quarters)
    slots = lax.all_to_all(slots.reshape(128, 1, 128), GROUP, 0, 0, tiled=True)
    correction, coarse = pl.pallas_call(
        unpack_kernel,
        out_shape=(
            jax.ShapeDtypeStruct((80, 128), F32),
            jax.ShapeDtypeStruct((40, 128), F32),
        ),
        in_specs=[smem, vmem],
        out_specs=(vmem, vmem),
        name="unpack",
    )(meta, slots.reshape(128, 128))
    return correction.reshape(5, 4, 2, 2, 128), coarse[:, :8].reshape(5, 4, 2, 8)


def solution(mesh):
    split = Mesh(mesh.devices.reshape(8, 2, 2, 8, 2), ("cy", "xh", "xl", "z", "c"))
    gy = ("cy", "xh", "xl")
    gz = ("z", "c")
    return jax.shard_map(
        on_device,
        mesh=split,
        in_specs=(
            P(None, None, gy, gz, None),
            P(None, gy, gz, None),
            P(None, None, None, gy, gz, None),
            P(None, None, None, gy, gz, None),
            P(None, None, None, gy, gz, None),
            P(None, None, None, None, gy, gz, None),
            P(None, None, None, None, gy, gz, None),
            P(gy, gz),
        ),
        out_specs=(P(None, None, gy, gz, None), P(None, None, gy, gz)),
        check_vma=False,
    )
```

time: 1850 us -> 274 us (0.15); the launches traced: 1820 us -> 273 us
  starting transfers between devices: 1110 us -> 17 us
  waiting for transfers between devices: 631 us -> 26.6 us
  Pallas kernels: 0 us -> 137 us
  blocking collectives: 43.5 us -> 83.3 us
    ppermute x384 -> x3, starting transfers between devices: 1110 us -> 17 us  [the longest x1 7.71 us: on_device(): other_cx = lax.ppermute(other_x, 'c', SWAP)]
    ppermute x384 -> x3, waiting for transfers between devices: 631 us -> 26.6 us  [the longest x1 23.6 us: on_device(): other_x = lax.ppermute(mine, 'xl', SWAP)]
    pallas_call x0 -> x3, Pallas kernels: none -> 137 us  [the longest x1 134 us: on_device(): pl.pallas_call(main_kernel, out_shape=jax.ShapeDtypeStruct((128, 128), F3...]
    all_to_all x0 -> x2, blocking collectives: none -> 83.3 us  [the longest x1 58.7 us: on_device(): mine = lax.all_to_all(packed.reshape(128, 24, 128), GROUP, 0, 0, tiled=True)]
    unnamed x1 -> x0, blocking collectives: 43.5 us -> none
  transfers between devices with their start and end apart: 384 -> 3, of which waited for: 285 -> 2; matrix products, arithmetic and copies ran while one was open for 0% -> 0% of each run, Pallas kernels for 0% -> 0%
where the time goes in v1:
time: 274 us; the launch traced here: 273 us
  Pallas kernels  137 us (50%)
  blocking collectives  83.3 us (30%)
  waiting for transfers between devices  26.6 us (10%)
  starting transfers between devices  17 us (6%)
  local copies, waits for them, and re-layouts  8.41 us (3%)
    pallas_call x1, Pallas kernels, on_device(): pl.pallas_call(main_kernel, out_shape=jax.ShapeDtypeStruct((128, 128), F3...  134 us
    all_to_all x1, blocking collectives, on_device(): mine = lax.all_to_all(packed.reshape(128, 24, 128), GROUP, 0, 0, tiled=True)  58.7 us
    all_to_all x1, blocking collectives, on_device(): slots = lax.all_to_all(slots.reshape(128, 1, 128), GROUP, 0, 0, tiled=True)  24.6 us
    ppermute x1, waiting for transfers between devices, on_device(): other_x = lax.ppermute(mine, 'xl', SWAP)  23.6 us
    ppermute x1, starting transfers between devices, on_device(): other_cx = lax.ppermute(other_x, 'c', SWAP)  7.71 us
    ppermute x1, starting transfers between devices, on_device(): other_c = lax.ppermute(mine, 'c', SWAP)  7.08 us
    unnamed x22, local copies, waits for them, and re-layouts  6.29 us
  transfers between devices with their start and end apart: 3, of which 2 were waited for; matrix products, arithmetic and copies ran while one was open for 0% of the time, Pallas kernels for 0%

profile of v1, /device:TPU:1, one launch (start us, length us, event | category | flops | bytes accessed | tf_op | source)
XLA Modules:
  0.0 273.1 jit_solution(5831221723463727399)
XLA Ops:
  0.6 1.0 reshape.55.low_x
  1.7 1.0 reshape.56.up_x
  2.7 0.1 stack.31.meta
  2.8 0.0 copy-start.5
  2.8 0.0 copy-start
  2.8 1.0 copy-done
  3.8 0.0 copy-start.1
  3.8 1.0 copy-done.1
  4.8 0.0 copy-start.2
  4.8 0.9 copy-done.2
  5.7 0.0 copy-start.3
  5.7 0.8 copy-done.3
  6.5 0.0 copy-start.4
  6.5 0.7 copy-done.4
  7.2 0.7 copy-done.6
  7.9 1.3 pack.1
  9.1 58.7 %all_to_all.10 = f32[128,24,128]{2,1,0:T(8,128)S(1)} all-to-all(f32[128,24,128]{2,1,0:T(8,128)S(1)} %bitcast.22), channel_id=1, replica_groups=mesh['cy'=8,'xh'=2,'xl'=2,'z'=8,'c'=2] {'z','cy','xh'}, dimensions={0} | all-to-all | bytes 3145728 | tf_op jit(solution)/shard_map/all_to_all | solution.py:312
  67.8 0.0 copy-done.5
  67.8 2.2 collective-permute-start.1
  70.0 7.1 %collective-permute-start = (f32[128,24,128]{2,1,0:T(8,128)S(1)}, f32[128,24,128]{2,1,0:T(8,128)S(1)}, u32[]{:S(2)}, u32[]{:S(2)}) collective-permute-start(f32[128,24,128]{2,1,0:T(8,128)S(1)} %all_to_all.10), channel_id=1, source_target_pairs={{0,1},{1,0},{2,3},{3,2},{4,5},{5,4},{6,7},{7,6},{8,9},{9,8},{10,11... | collective-permute-start | bytes 4718600 | tf_op jit(solution)/shard_map/ppermute | solution.py:314
  77.1 23.6 %collective-permute-done.1 = f32[128,24,128]{2,1,0:T(8,128)S(1)} collective-permute-done((f32[128,24,128]{2,1,0:T(8,128)S(1)}, f32[128,24,128]{2,1,0:T(8,128)S(1)}, u32[]{:S(2)}, u32[]{:S(2)}) %collective-permute-start.1) | collective-permute-done | bytes 1572896 | tf_op jit(solution)/shard_map/ppermute | solution.py:313
  100.7 7.7 %collective-permute-start.2 = (f32[128,24,128]{2,1,0:T(8,128)S(1)}, f32[128,24,128]{2,1,0:T(8,128)S(1)}, u32[]{:S(2)}, u32[]{:S(2)}) collective-permute-start(f32[128,24,128]{2,1,0:T(8,128)S(1)} %collective-permute-done.1), channel_id=1, source_target_pairs={{0,1},{1,0},{2,3},{3,2},{4,5},{5,4},{6,7},{7,6},{8,9},{9,8},{10,11... | collective-permute-start | bytes 4718600 | tf_op jit(solution)/shard_map/ppermute | solution.py:315
  108.4 0.0 collective-permute-done
  108.4 0.0 copy-start.9
  108.4 3.0 %collective-permute-done.2 = f32[128,24,128]{2,1,0:T(8,128)S(1)} collective-permute-done((f32[128,24,128]{2,1,0:T(8,128)S(1)}, f32[128,24,128]{2,1,0:T(8,128)S(1)}, u32[]{:S(2)}, u32[]{:S(2)}) %collective-permute-start.2) | collective-permute-done | bytes 1572896 | tf_op jit(solution)/shard_map/ppermute | solution.py:315
  111.4 0.0 copy-done.9
  111.4 1.2 copy-done.10
  112.6 0.0 copy-done.7
  112.6 0.0 copy-done.8
  112.6 134.2 %sweeps.1 = f32[128,128]{1,0:T(8,128)} custom-call(s32[5]{0:T(128)} %copy-done.5, f32[8,16,24,128]{3,2,1,0:T(8,128)} %bitcast.28, f32[8,16,24,128]{3,2,1,0:T(8,128)} %bitcast.30, f32[8,16,24,128]{3,2,1,0:T(8,128)} %bitcast.29, f32[8,16,24,128]{3,2,1,0:T(8,128)} %bitcast.31), custom_call_target="tpu_custom_call" | custom-call | tf_op jit(solution)/shard_map/sweeps/pallas_call | solution.py:318
  246.9 24.6 %all_to_all.11 = f32[128,1,128]{2,1,0:T(1,128)} all-to-all(f32[128,1,128]{2,1,0:T(1,128)} %bitcast.32), channel_id=1, replica_groups=mesh['cy'=8,'xh'=2,'xl'=2,'z'=8,'c'=2] {'z','cy','xh'}, dimensions={0} | all-to-all | bytes 131072 | tf_op jit(solution)/shard_map/all_to_all | solution.py:342
  271.5 1.6 unpack.1
  (4 shorter events, 0.0 us)
Async XLA Ops:
  2.8 65.0 %copy-start.5 = (s32[5]{0:T(128)}, s32[5]{0:T(128)S(1)}, u32[]{:S(2)}) copy-start(s32[5]{0:T(128)S(1)} %stack.31.meta) | copy-start | bytes 64
  2.8 1.0 copy-start
  3.8 1.0 copy-start.1
  4.8 0.9 copy-start.2
  5.7 0.8 copy-start.3
  6.5 0.7 copy-start.4
  7.2 0.7 copy-start.6
  67.8 44.8 %copy-start.7 = (f32[128,24,128]{2,1,0:T(8,128)}, f32[128,24,128]{2,1,0:T(8,128)S(1)}, u32[]{:S(2)}) copy-start(f32[128,24,128]{2,1,0:T(8,128)S(1)} %all_to_all.10) | copy-start | bytes 4718596
  67.8 32.9 %collective-permute-start.1 = (f32[128,24,128]{2,1,0:T(8,128)S(1)}, f32[128,24,128]{2,1,0:T(8,128)S(1)}, u32[]{:S(2)}, u32[]{:S(2)}) collective-permute-start(f32[128,24,128]{2,1,0:T(8,128)S(1)} %all_to_all.10), channel_id=1, source_target_pairs={{0,16},{16,0},{1,17},{17,1},{2,18},{18,2},{3,19},{19,3},{4,20},{20... | collective-permute-start | bytes 4718600 | tf_op jit(solution)/shard_map/ppermute | solution.py:313
  70.0 38.4 %collective-permute-start = (f32[128,24,128]{2,1,0:T(8,128)S(1)}, f32[128,24,128]{2,1,0:T(8,128)S(1)}, u32[]{:S(2)}, u32[]{:S(2)}) collective-permute-start(f32[128,24,128]{2,1,0:T(8,128)S(1)} %all_to_all.10), channel_id=1, source_target_pairs={{0,1},{1,0},{2,3},{3,2},{4,5},{5,4},{6,7},{7,6},{8,9},{9,8},{10,11... | collective-permute-start | bytes 4718600 | tf_op jit(solution)/shard_map/ppermute | solution.py:314
  100.7 11.9 %copy-start.8 = (f32[128,24,128]{2,1,0:T(8,128)}, f32[128,24,128]{2,1,0:T(8,128)S(1)}, u32[]{:S(2)}) copy-start(f32[128,24,128]{2,1,0:T(8,128)S(1)} %collective-permute-done.1) | copy-start | bytes 4718596
  100.7 10.7 %collective-permute-start.2 = (f32[128,24,128]{2,1,0:T(8,128)S(1)}, f32[128,24,128]{2,1,0:T(8,128)S(1)}, u32[]{:S(2)}, u32[]{:S(2)}) collective-permute-start(f32[128,24,128]{2,1,0:T(8,128)S(1)} %collective-permute-done.1), channel_id=1, source_target_pairs={{0,1},{1,0},{2,3},{3,2},{4,5},{5,4},{6,7},{7,6},{8,9},{9,8},{10,11... | collective-permute-start | bytes 4718600 | tf_op jit(solution)/shard_map/ppermute | solution.py:315
  108.4 3.0 %copy-start.9 = (f32[128,24,128]{2,1,0:T(8,128)}, f32[128,24,128]{2,1,0:T(8,128)S(1)}, u32[]{:S(2)}) copy-start(f32[128,24,128]{2,1,0:T(8,128)S(1)} %collective-permute-done) | copy-start | bytes 4718596
  111.4 1.2 copy-start.10

commit v2 on v1

--- a/solution.py
+++ b/solution.py
@@ -10,6 +10,8 @@
 NY = 64
 DIAGS = NY + NZ - 1
 PITCH = 272
+ROWS = 145
+WIDTH = 321
 SWAP = [(0, 1), (1, 0)]
 GROUP = ("z", "cy", "xh")
 SMEM = pltpu.SMEM
@@ -73,15 +75,21 @@
 
 
 def column(ref, d, base, j):
-    return ref[d, pl.ds(base + j, 8, stride=5), :]
-
-
-def row(ref, d, r):
-    return jnp.broadcast_to(ref[d, pl.ds(r, 1), :], (8, 128))
+    return ref[pl.ds(ROWS * d + base + j, 8, stride=5), :]
+
+
+def matmul(left, right):
+    return [
+        [tree([left[o][i] * right[i][j] for i in range(5)]) for j in range(5)] for o in range(5)
+    ]
+
+
+def turned(block, by):
+    return [[pltpu.roll(v, by, 1) for v in line] for line in block]
 
 
 def main_kernel(
-    meta, q0, q1, q2, q3, out, df, du, tf, tu, tmp, al, au, g, vv, f1, c1, rl, ru, sem
+    meta, q0, q1, q2, q3, out, df, du, tf, tu, tmp, al, au, g, vv, f1, c1, change, full, sem
 ):
     core = meta[0]
     side = meta[1]
@@ -110,77 +118,111 @@
         block = jnp.concatenate(
             [fl[pl.ds(4 * d + p, 32, stride=PITCH - 4), :] for p in range(4)], axis=0
         )
-        tf[d, pl.ds(0, 128), :] = block.T
+        tf[pl.ds(ROWS * d, 128), :] = block.T
         return carry
 
     lax.fori_loop(0, DIAGS, turn_f, 0, unroll=5)
 
-    def turn_u(e, carry):
-        for p in range(4):
-            for jz in range(2):
-                tmp[pl.ds(p * 32 + jz, 16, stride=2), :] = ul[
-                    pl.ds(8 * e + jz * 4 + p, 16, stride=PITCH - 8), :
-                ]
-        tu[pl.ds(pl.multiple_of(128 * e + 128, 128), 128), :] = tmp[...].T
+    def turn_u(n, carry):
+        for k in range(4):
+            e = 4 * n + k
+            for p in range(4):
+                for jz in range(2):
+                    tmp[k, pl.ds(p * 32 + jz, 16, stride=2), :] = ul[
+                        pl.ds(8 * e + jz * 4 + p, 16, stride=PITCH - 8), :
+                    ]
+            tu[pl.ds(pl.multiple_of(128 * e + 128, 128), 128), :] = tmp[k].T
         return carry
 
-    lax.fori_loop(0, 47, turn_u, 0)
-
-    def prepare(d, carry):
-        piv = [column(tf, d, 0, i) for i in range(5)]
-        pl_cols = [tree([piv[i] * row(tf, d, 25 + 5 * i + j) for i in range(5)]) for j in range(5)]
-        pu_cols = [tree([piv[i] * row(tf, d, 50 + 5 * i + j) for i in range(5)]) for j in range(5)]
-
-        def times(left, right):
-            return [tree([left[i] * spread(right[j], i) for i in range(5)]) for j in range(5)]
-
-        def shifted(cols, by):
-            return [pltpu.roll(v, by, 1) for v in cols]
-
+    lax.fori_loop(0, 12, turn_u, 0)
+
+    def lower_rows(k, r):
+        return tf[pl.ds(ROWS * 8 * k + r, 8, stride=ROWS), :]
+
+    def upper_rows(k, r):
+        even = tu[pl.ds(64 * 8 * k + 128 + r, 8, stride=64), :]
+        odd = tu[pl.ds(64 * 8 * k + 64 + r, 8, stride=64), :]
+        return jnp.where(even_z, even, odd)
+
+    def invert(k, slot):
+        piv, before, after = (
+            [[lower_rows(k, 25 * n + 5 * o + i) for i in range(5)] for o in range(5)]
+            for n in range(3)
+        )
+        back = matmul(piv, before)
+        ahead = matmul(piv, after)
         w = [piv]
         for _ in range(3):
-            w.append([-v for v in times(pl_cols, shifted(w[-1], 32))])
+            w.append([[-v for v in line] for line in matmul(back, turned(w[-1], 32))])
         inverse = {3: w[3]}
         for s in (2, 1, 0, -1, -2, -3):
-            below = times(pu_cols, shifted(inverse[s + 1], 96))
-            inverse[s] = [w[s][j] - below[j] if s >= 0 else -below[j] for j in range(5)]
-        full = [inverse[0]] + [
-            [a + b for a, b in zip(inverse[s], inverse[s - 4])] for s in (1, 2, 3)
-        ]
-        for k in range(7):
-            v = tf[d, pl.ds(72 + 8 * k, 8), :]
-            for s in range(4):
-                rl[s, pl.ds(8 * k, 8), :] = v if s == 0 else pltpu.roll(v, 32 * s, 1)
-        for k in range(8):
-            even = tu[pl.ds(pl.multiple_of(64 * d + 128, 64) + 8 * k, 8), :]
-            odd = tu[pl.ds(pl.multiple_of(64 * d + 64, 64) + 8 * k, 8), :]
-            v = jnp.where(even_z, even, odd)
-            for s in range(4):
-                ru[s, pl.ds(8 * k, 8), :] = v if s == 0 else pltpu.roll(v, 32 * s, 1)
+            below = matmul(ahead, turned(inverse[s + 1], 96))
+            inverse[s] = [
+                [(w[s][o][j] - below[o][j]) if s >= 0 else -below[o][j] for j in range(5)]
+                for o in range(5)
+            ]
         for s in range(4):
-            for n, (dest, source, base) in enumerate(
-                ((al, rl, 3), (al, rl, 28), (au, ru, 0), (au, ru, 25))
+            for o in range(5):
+                for i in range(5):
+                    v = inverse[s][o][i]
+                    if s > 0:
+                        v = v + inverse[s - 4][o][i]
+                    full[slot, s * 25 + o * 5 + i] = v
+
+    def couple(k, slot):
+        totals = [[] for _ in range(5)]
+        for s in range(4):
+            inverse = [[full[slot, s * 25 + o * 5 + i] for i in range(5)] for o in range(5)]
+
+            def moved(v, s=s):
+                return v if s == 0 else pltpu.roll(v, 32 * s, 1)
+
+            for n, (dest, rows, base) in enumerate(
+                (
+                    (al, lower_rows, 75),
+                    (al, lower_rows, 100),
+                    (au, upper_rows, 0),
+                    (au, upper_rows, 25),
+                )
             ):
                 for j in range(5):
-                    dest[d, pl.ds(8 * (s * 10 + 5 * (n % 2) + j), 8), :] = tree(
-                        [full[s][i] * row(source, s, base + 5 * i + j) for i in range(5)]
-                    )
-        g[d] = tree([full[s][i] * row(ru, s, 50 + i) for s in range(4) for i in range(5)])
-        vv[d] = row(ru, 0, 55)
+                    terms = [moved(rows(k, base + 5 * i + j)) for i in range(5)]
+                    at = WIDTH * 8 * k + 8 * (s * 10 + 5 * (n % 2) + j)
+                    for o in range(5):
+                        dest[pl.ds(at + o, 8, stride=WIDTH), :] = tree(
+                            [inverse[o][i] * terms[i] for i in range(5)]
+                        )
+            terms = [moved(upper_rows(k, 50 + i)) for i in range(5)]
+            for o in range(5):
+                totals[o].append(tree([inverse[o][i] * terms[i] for i in range(5)]))
+        for o in range(5):
+            g[pl.ds(64 * k + o, 8, stride=8), :] = tree(totals[o])
+        vv[pl.ds(pl.multiple_of(8 * k, 8), 8), :] = upper_rows(k, 55)
+
+    invert(0, 0)
+
+    def prepare(k, carry):
+        couple(k - 1, (k - 1) % 2)
+        invert(k, k % 2)
         return carry
 
-    lax.fori_loop(0, DIAGS, prepare, 0)
+    lax.fori_loop(1, 12, prepare, 0)
+    couple(11, 1)
 
     def product(ref, d, f, step):
         terms = []
+        start = WIDTH * d
         for s in range(4):
             by_y = f if s == 0 else pltpu.roll(f, 32 * s, 1)
             by_z = pltpu.roll(f, (32 * s + step) % 128, 1)
             for i in range(5):
-                terms.append(ref[d, pl.ds(8 * (s * 10 + i), 8), :] * spread(by_y, i))
+                terms.append(ref[pl.ds(start + 8 * (s * 10 + i), 8), :] * spread(by_y, i))
             for i in range(5):
-                terms.append(ref[d, pl.ds(8 * (s * 10 + 5 + i), 8), :] * spread(by_z, i))
+                terms.append(ref[pl.ds(start + 8 * (s * 10 + 5 + i), 8), :] * spread(by_z, i))
         return tree(terms)
+
+    def tile(d):
+        return pl.ds(pl.multiple_of(8 * d, 8), 8)
 
     def inside(d):
         return (z <= d) & (z >= d - (NY - 1))
@@ -188,7 +230,7 @@
     nothing = jnp.zeros((8, 128), F32)
 
     def forward_first(d, f):
-        f = jnp.where(inside(d), g[d] - product(al, d, f, 1), 0.0)
+        f = jnp.where(inside(d), g[tile(d), :] - product(al, d, f, 1), 0.0)
         f1[d] = f
         return f
 
@@ -199,14 +241,14 @@
         coupled = product(au, d, f, -1)
         f = jnp.where(inside(d), f1[d] - coupled, 0.0)
         f1[d] = f
-        g[d] = coupled
+        g[tile(d), :] = coupled
         return f
 
     lax.fori_loop(0, DIAGS, backward_first, nothing)
 
     def forward_second(d, f):
         coupled = product(al, d, f, 1)
-        f = jnp.where(inside(d), -(g[d] + coupled), 0.0)
+        f = jnp.where(inside(d), -(g[tile(d), :] + coupled), 0.0)
         c1[d] = coupled
         return f
 
@@ -217,29 +259,28 @@
         coupled = product(au, d, f, -1)
         f = jnp.where(inside(d), -(c1[d] + coupled), 0.0)
         f1[d] = f1[d] + f
-        c1[d] = jnp.where(inside(d), coupled, 0.0)
+        change[tile(d + 1), :] = jnp.where(inside(d), coupled, 0.0)
         return f
 
+    change[0:8, :] = nothing
     lax.fori_loop(0, DIAGS, backward_second, nothing)
 
-    def residual(d, before):
+    def residual(d, carry):
+        before = change[tile(d), :]
         by_z = pltpu.roll(before, 1, 1)
-        g[d] = vv[d] * tree(
+        g[tile(d), :] = vv[pl.ds(d, 1), :] * tree(
             [column(tf, d, 75, i) * spread(before, i) for i in range(5)]
             + [column(tf, d, 100, i) * spread(by_z, i) for i in range(5)]
         )
-        return c1[d]
-
-    lax.fori_loop(0, DIAGS, residual, nothing)
+        return carry
+
+    lax.fori_loop(0, DIAGS, residual, 0, unroll=5)
     for bit, length in ((16, 79), (8, 71), (4, 67), (2, 65), (1, 64)):
-
-        def straighten(d, carry, bit=bit):
-            far = (z & bit) != 0
+        far = (z & bit) != 0
+        for d in range(length):
             f1[d] = jnp.where(far, f1[d + bit], f1[d])
-            g[d] = jnp.where(far, g[d + bit], g[d])
-            return carry
-
-        lax.fori_loop(0, length, straighten, 0)
+            here, there = pl.ds(8 * d, 8), pl.ds(8 * (d + bit), 8)
+            g[here, :] = jnp.where(far, g[there, :], g[here, :])
 
     owner_y = lane & 15
     owner_z = lane >> 4
@@ -249,7 +290,7 @@
         for jy in range(2):
             y = 4 * n + 2 * side + jy
             value = f1[y]
-            total = g[y]
+            total = g[tile(y), :]
             for by in (16, 8, 4, 2, 1):
                 total = total + pltpu.roll(total, 128 - by, 1)
             for jz in range(2):
@@ -261,7 +302,7 @@
                     sums[k] = jnp.where(owner_y == n, picked, sums[k])
         return tuple(sums)
 
-    slots = lax.fori_loop(0, 16, collect, (nothing,) * 16)
+    slots = lax.fori_loop(0, 16, collect, (nothing,) * 16, unroll=4)
     out[...] = jnp.concatenate(slots, axis=0).T
 
 
@@ -323,17 +364,17 @@
         scratch_shapes=[
             pltpu.VMEM((8, 2, 2, 17, 2, 8, 128), F32),
             pltpu.VMEM((8, 2, 17, 2, 8, 128), F32),
-            pltpu.VMEM((DIAGS, 144, 128), F32),
+            pltpu.VMEM((96 * ROWS, 128), F32),
             pltpu.VMEM((50 * 128, 128), F32),
-            pltpu.VMEM((128, 128), F32),
-            pltpu.VMEM((DIAGS, 320, 128), F32),
-            pltpu.VMEM((DIAGS, 320, 128), F32),
+            pltpu.VMEM((4, 128, 128), F32),
+            pltpu.VMEM((96 * WIDTH, 128), F32),
+            pltpu.VMEM((96 * WIDTH, 128), F32),
+            pltpu.VMEM((96 * 8, 128), F32),
+            pltpu.VMEM((96, 128), F32),
             diag,
             diag,
-            diag,
-            diag,
-            pltpu.VMEM((4, 56, 128), F32),
-            pltpu.VMEM((4, 64, 128), F32),
+            pltpu.VMEM((97 * 8, 128), F32),
+            pltpu.VMEM((2, 100, 8, 128), F32),
             pltpu.SemaphoreType.DMA((12,)),
         ],
         compiler_params=pltpu.CompilerParams(vmem_limit_bytes=60 << 20),

time: 274 us -> 210 us (0.77)
  Pallas kernels: 137 us -> 73.4 us
    pallas_call x1, Pallas kernels: 134 us -> 70.5 us  [on_device(): pl.pallas_call(main_kernel, out_shape=jax.ShapeDtypeStruct((128, 128), F3...]
where the time goes in v2:
time: 210 us; the launch traced here: 209 us
  blocking collectives  83.3 us (40%)
  Pallas kernels  73.4 us (35%)
  waiting for transfers between devices  26.6 us (13%)
  starting transfers between devices  17 us (8%)
  local copies, waits for them, and re-layouts  8.41 us (4%)
    pallas_call x1, Pallas kernels, on_device(): pl.pallas_call(main_kernel, out_shape=jax.ShapeDtypeStruct((128, 128), F3...  70.5 us
    all_to_all x1, blocking collectives, on_device(): mine = lax.all_to_all(packed.reshape(128, 24, 128), GROUP, 0, 0, tiled=True)  58.7 us
    all_to_all x1, blocking collectives, on_device(): slots = lax.all_to_all(slots.reshape(128, 1, 128), GROUP, 0, 0, tiled=True)  24.6 us
    ppermute x1, waiting for transfers between devices, on_device(): other_x = lax.ppermute(mine, 'xl', SWAP)  23.6 us
    ppermute x1, starting transfers between devices, on_device(): other_cx = lax.ppermute(other_x, 'c', SWAP)  7.71 us
    ppermute x1, starting transfers between devices, on_device(): other_c = lax.ppermute(mine, 'c', SWAP)  7.08 us
    unnamed x22, local copies, waits for them, and re-layouts  6.29 us
  transfers between devices with their start and end apart: 3, of which 2 were waited for; matrix products, arithmetic and copies ran while one was open for 0% of the time, Pallas kernels for 0%

profile of v2, /device:TPU:1, one launch (start us, length us, event | category | flops | bytes accessed | tf_op | source)
XLA Modules:
  0.0 209.4 jit_solution(7946521312561684090)
XLA Ops:
  0.6 1.0 reshape.55.low_x
  1.7 1.0 reshape.56.up_x
  2.7 0.1 stack.31.meta
  2.8 0.0 copy-start.5
  2.8 0.0 copy-start
  2.8 1.0 copy-done
  3.8 0.0 copy-start.1
  3.8 1.0 copy-done.1
  4.8 0.0 copy-start.2
  4.8 0.9 copy-done.2
  5.7 0.0 copy-start.3
  5.7 0.8 copy-done.3
  6.5 0.0 copy-start.4
  6.5 0.7 copy-done.4
  7.2 0.7 copy-done.6
  7.9 1.3 pack.1
  9.1 58.7 %all_to_all.10 = f32[128,24,128]{2,1,0:T(8,128)S(1)} all-to-all(f32[128,24,128]{2,1,0:T(8,128)S(1)} %bitcast.22), channel_id=1, replica_groups=mesh['cy'=8,'xh'=2,'xl'=2,'z'=8,'c'=2] {'z','cy','xh'}, dimensions={0} | all-to-all | bytes 3145728 | tf_op jit(solution)/shard_map/all_to_all | solution.py:353
  67.8 0.0 copy-done.5
  67.8 2.2 %collective-permute-start.1 = (f32[128,24,128]{2,1,0:T(8,128)S(1)}, f32[128,24,128]{2,1,0:T(8,128)S(1)}, u32[]{:S(2)}, u32[]{:S(2)}) collective-permute-start(f32[128,24,128]{2,1,0:T(8,128)S(1)} %all_to_all.10), channel_id=1, source_target_pairs={{0,16},{16,0},{1,17},{17,1},{2,18},{18,2},{3,19},{19,3},{4,20},{20... | collective-permute-start | bytes 4718600 | tf_op jit(solution)/shard_map/ppermute | solution.py:354
  70.0 7.1 %collective-permute-start = (f32[128,24,128]{2,1,0:T(8,128)S(1)}, f32[128,24,128]{2,1,0:T(8,128)S(1)}, u32[]{:S(2)}, u32[]{:S(2)}) collective-permute-start(f32[128,24,128]{2,1,0:T(8,128)S(1)} %all_to_all.10), channel_id=1, source_target_pairs={{0,1},{1,0},{2,3},{3,2},{4,5},{5,4},{6,7},{7,6},{8,9},{9,8},{10,11... | collective-permute-start | bytes 4718600 | tf_op jit(solution)/shard_map/ppermute | solution.py:355
  77.1 23.6 %collective-permute-done.1 = f32[128,24,128]{2,1,0:T(8,128)S(1)} collective-permute-done((f32[128,24,128]{2,1,0:T(8,128)S(1)}, f32[128,24,128]{2,1,0:T(8,128)S(1)}, u32[]{:S(2)}, u32[]{:S(2)}) %collective-permute-start.1) | collective-permute-done | bytes 1572896 | tf_op jit(solution)/shard_map/ppermute | solution.py:354
  100.7 7.7 %collective-permute-start.2 = (f32[128,24,128]{2,1,0:T(8,128)S(1)}, f32[128,24,128]{2,1,0:T(8,128)S(1)}, u32[]{:S(2)}, u32[]{:S(2)}) collective-permute-start(f32[128,24,128]{2,1,0:T(8,128)S(1)} %collective-permute-done.1), channel_id=1, source_target_pairs={{0,1},{1,0},{2,3},{3,2},{4,5},{5,4},{6,7},{7,6},{8,9},{9,8},{10,11... | collective-permute-start | bytes 4718600 | tf_op jit(solution)/shard_map/ppermute | solution.py:356
  108.4 0.0 collective-permute-done
  108.4 0.0 copy-start.9
  108.4 3.0 %collective-permute-done.2 = f32[128,24,128]{2,1,0:T(8,128)S(1)} collective-permute-done((f32[128,24,128]{2,1,0:T(8,128)S(1)}, f32[128,24,128]{2,1,0:T(8,128)S(1)}, u32[]{:S(2)}, u32[]{:S(2)}) %collective-permute-start.2) | collective-permute-done | bytes 1572896 | tf_op jit(solution)/shard_map/ppermute | solution.py:356
  111.4 0.0 copy-done.9
  111.4 1.2 copy-done.10
  112.6 0.0 copy-done.7
  112.6 0.0 copy-done.8
  112.6 70.5 %sweeps.1 = f32[128,128]{1,0:T(8,128)} custom-call(s32[5]{0:T(128)} %copy-done.5, f32[8,16,24,128]{3,2,1,0:T(8,128)} %bitcast.28, f32[8,16,24,128]{3,2,1,0:T(8,128)} %bitcast.30, f32[8,16,24,128]{3,2,1,0:T(8,128)} %bitcast.29, f32[8,16,24,128]{3,2,1,0:T(8,128)} %bitcast.31), custom_call_target="tpu_custom_call" | custom-call | tf_op jit(solution)/shard_map/sweeps/pallas_call | solution.py:359
  183.2 24.6 %all_to_all.11 = f32[128,1,128]{2,1,0:T(1,128)} all-to-all(f32[128,1,128]{2,1,0:T(1,128)} %bitcast.32), channel_id=1, replica_groups=mesh['cy'=8,'xh'=2,'xl'=2,'z'=8,'c'=2] {'z','cy','xh'}, dimensions={0} | all-to-all | bytes 131072 | tf_op jit(solution)/shard_map/all_to_all | solution.py:383
  207.8 1.6 unpack.1
  (4 shorter events, 0.0 us)
Async XLA Ops:
  2.8 65.0 %copy-start.5 = (s32[5]{0:T(128)}, s32[5]{0:T(128)S(1)}, u32[]{:S(2)}) copy-start(s32[5]{0:T(128)S(1)} %stack.31.meta) | copy-start | bytes 64
  2.8 1.0 copy-start
  3.8 1.0 copy-start.1
  4.8 0.9 copy-start.2
  5.7 0.8 copy-start.3
  6.5 0.7 copy-start.4
  7.2 0.7 copy-start.6
  67.8 44.8 %copy-start.7 = (f32[128,24,128]{2,1,0:T(8,128)}, f32[128,24,128]{2,1,0:T(8,128)S(1)}, u32[]{:S(2)}) copy-start(f32[128,24,128]{2,1,0:T(8,128)S(1)} %all_to_all.10) | copy-start | bytes 4718596
  67.8 32.9 %collective-permute-start.1 = (f32[128,24,128]{2,1,0:T(8,128)S(1)}, f32[128,24,128]{2,1,0:T(8,128)S(1)}, u32[]{:S(2)}, u32[]{:S(2)}) collective-permute-start(f32[128,24,128]{2,1,0:T(8,128)S(1)} %all_to_all.10), channel_id=1, source_target_pairs={{0,16},{16,0},{1,17},{17,1},{2,18},{18,2},{3,19},{19,3},{4,20},{20... | collective-permute-start | bytes 4718600 | tf_op jit(solution)/shard_map/ppermute | solution.py:354
  70.0 38.4 %collective-permute-start = (f32[128,24,128]{2,1,0:T(8,128)S(1)}, f32[128,24,128]{2,1,0:T(8,128)S(1)}, u32[]{:S(2)}, u32[]{:S(2)}) collective-permute-start(f32[128,24,128]{2,1,0:T(8,128)S(1)} %all_to_all.10), channel_id=1, source_target_pairs={{0,1},{1,0},{2,3},{3,2},{4,5},{5,4},{6,7},{7,6},{8,9},{9,8},{10,11... | collective-permute-start | bytes 4718600 | tf_op jit(solution)/shard_map/ppermute | solution.py:355
  100.7 11.9 %copy-start.8 = (f32[128,24,128]{2,1,0:T(8,128)}, f32[128,24,128]{2,1,0:T(8,128)S(1)}, u32[]{:S(2)}) copy-start(f32[128,24,128]{2,1,0:T(8,128)S(1)} %collective-permute-done.1) | copy-start | bytes 4718596
  100.7 10.7 %collective-permute-start.2 = (f32[128,24,128]{2,1,0:T(8,128)S(1)}, f32[128,24,128]{2,1,0:T(8,128)S(1)}, u32[]{:S(2)}, u32[]{:S(2)}) collective-permute-start(f32[128,24,128]{2,1,0:T(8,128)S(1)} %collective-permute-done.1), channel_id=1, source_target_pairs={{0,1},{1,0},{2,3},{3,2},{4,5},{5,4},{6,7},{7,6},{8,9},{9,8},{10,11... | collective-permute-start | bytes 4718600 | tf_op jit(solution)/shard_map/ppermute | solution.py:356
  108.4 3.0 %copy-start.9 = (f32[128,24,128]{2,1,0:T(8,128)}, f32[128,24,128]{2,1,0:T(8,128)S(1)}, u32[]{:S(2)}) copy-start(f32[128,24,128]{2,1,0:T(8,128)S(1)} %collective-permute-done) | copy-start | bytes 4718596
  111.4 1.2 copy-start.10

commit v3 on v2

--- a/solution.py
+++ b/solution.py
@@ -1,3 +1,5 @@
+from itertools import chain
+
 import jax
 import jax.numpy as jnp
 from jax import lax
@@ -12,6 +14,7 @@
 PITCH = 272
 ROWS = 145
 WIDTH = 321
+SHARE = 13
 SWAP = [(0, 1), (1, 0)]
 GROUP = ("z", "cy", "xh")
 SMEM = pltpu.SMEM
@@ -32,7 +35,28 @@
     return jnp.broadcast_to(value[i : i + 1, :], (8, 128))
 
 
-def pack_kernel(meta, vol, rhs, codes, piv, low_x, up_x, low, up, out, tile):
+def pack_kernel(
+    meta, vol, rhs_in, codes_in, piv_in, low_x_in, up_x_in, low_in, up_in, out,
+    rhs, codes, piv, low_x, up_x, low, up, tile, sem,
+):
+    copies = [
+        pltpu.make_async_copy(src, dst, sem.at[n])
+        for n, (src, dst) in enumerate(
+            (
+                (piv_in, piv),
+                (low_x_in, low_x),
+                (up_x_in, up_x),
+                (low_in, low),
+                (up_in, up),
+                (rhs_in, rhs),
+                (codes_in, codes),
+            )
+        )
+    ]
+    for copy in copies:
+        copy.start()
+    for copy in copies:
+        copy.wait()
     first_z = meta[2]
     last_z = meta[3]
     zero = jnp.zeros((25, 128), F32)
@@ -43,8 +67,8 @@
                 at = p * 4 + jy * 2 + jz
                 t = tile.at[(jy * 4 + p) % 2]
                 t[0:25, :] = piv[pl.ds(at, 25, stride=16), :]
-                t[25:50, :] = low_x[pl.ds(at - 4, 25, stride=12), :] if p > 0 else zero
-                t[50:75, :] = up_x[pl.ds(at, 25, stride=12), :] if p < 3 else zero
+                t[25:50, :] = low_x[pl.ds(2 * p - 2 + jy, 25, stride=6), jz, :] if p > 0 else zero
+                t[50:75, :] = up_x[pl.ds(2 * p + jy, 25, stride=6), jz, :] if p < 3 else zero
                 t[75:100, :] = low[pl.ds(at, 25, stride=16), :]
                 along_z = low[pl.ds(400 + at, 25, stride=16), :]
                 if jz == 0:
@@ -78,10 +102,22 @@
     return ref[pl.ds(ROWS * d + base + j, 8, stride=5), :]
 
 
-def matmul(left, right):
-    return [
-        [tree([left[o][i] * right[i][j] for i in range(5)]) for j in range(5)] for o in range(5)
-    ]
+def matmul(left, right, into):
+    for o in range(5):
+        into.append([tree([left[o][i] * right[i][j] for i in range(5)]) for j in range(5)])
+        yield
+
+
+def mixed(*works):
+    works = list(works)
+    while works:
+        for work in list(works):
+            try:
+                next(work)
+            except StopIteration:
+                works.remove(work)
+                continue
+            yield
 
 
 def turned(block, by):
@@ -89,7 +125,7 @@
 
 
 def main_kernel(
-    meta, q0, q1, q2, q3, out, df, du, tf, tu, tmp, al, au, g, vv, f1, c1, change, full, sem
+    meta, q0, q1, q2, q3, out, df, du, tf, tu, tmp, al0, al1, au0, au1, g0, g1, h, vv, f1, c1, change, full0, full1, sem
 ):
     core = meta[0]
     side = meta[1]
@@ -144,19 +180,26 @@
         odd = tu[pl.ds(64 * 8 * k + 64 + r, 8, stride=64), :]
         return jnp.where(even_z, even, odd)
 
-    def invert(k, slot):
+    al, au, g, full = (al0, al1), (au0, au1), (g0, g1), (full0, full1)
+
+    def invert(n, half):
+        k = 2 * n + half
         piv, before, after = (
-            [[lower_rows(k, 25 * n + 5 * o + i) for i in range(5)] for o in range(5)]
-            for n in range(3)
+            [[lower_rows(k, 25 * m + 5 * o + i) for i in range(5)] for o in range(5)]
+            for m in range(3)
         )
-        back = matmul(piv, before)
-        ahead = matmul(piv, after)
+        back, ahead = [], []
+        yield from matmul(piv, before, back)
+        yield from matmul(piv, after, ahead)
         w = [piv]
         for _ in range(3):
-            w.append([[-v for v in line] for line in matmul(back, turned(w[-1], 32))])
+            product_now = []
+            yield from matmul(back, turned(w[-1], 32), product_now)
+            w.append([[-v for v in line] for line in product_now])
         inverse = {3: w[3]}
         for s in (2, 1, 0, -1, -2, -3):
-            below = matmul(ahead, turned(inverse[s + 1], 96))
+            below = []
+            yield from matmul(ahead, turned(inverse[s + 1], 96), below)
             inverse[s] = [
                 [(w[s][o][j] - below[o][j]) if s >= 0 else -below[o][j] for j in range(5)]
                 for o in range(5)
@@ -167,51 +210,48 @@
                     v = inverse[s][o][i]
                     if s > 0:
                         v = v + inverse[s - 4][o][i]
-                    full[slot, s * 25 + o * 5 + i] = v
-
-    def couple(k, slot):
+                    full[half][n, s * 25 + o * 5 + i] = v
+
+    def couple(n, half, dest, rows, base):
+        k = 2 * n + half
+        for s in range(4):
+            inverse = [[full[half][n, s * 25 + o * 5 + i] for i in range(5)] for o in range(5)]
+            for m in range(2):
+                for j in range(5):
+                    terms = [rows(k, base + 25 * m + 5 * i + j) for i in range(5)]
+                    if s > 0:
+                        terms = [pltpu.roll(v, 32 * s, 1) for v in terms]
+                    at = WIDTH * 8 * n + 8 * (s * 10 + 5 * m + j)
+                    for o in range(5):
+                        dest[half][pl.ds(at + o, 8, stride=WIDTH), :] = tree(
+                            [inverse[o][i] * terms[i] for i in range(5)]
+                        )
+                    yield
+
+    def couple_lower(n, half):
+        return couple(n, half, al, lower_rows, 75)
+
+    def couple_upper(n, half):
+        return couple(n, half, au, upper_rows, 0)
+
+    def start_values(n, half):
+        k = 2 * n + half
         totals = [[] for _ in range(5)]
         for s in range(4):
-            inverse = [[full[slot, s * 25 + o * 5 + i] for i in range(5)] for o in range(5)]
-
-            def moved(v, s=s):
-                return v if s == 0 else pltpu.roll(v, 32 * s, 1)
-
-            for n, (dest, rows, base) in enumerate(
-                (
-                    (al, lower_rows, 75),
-                    (al, lower_rows, 100),
-                    (au, upper_rows, 0),
-                    (au, upper_rows, 25),
+            terms = [upper_rows(k, 50 + i) for i in range(5)]
+            if s > 0:
+                terms = [pltpu.roll(v, 32 * s, 1) for v in terms]
+            for o in range(5):
+                totals[o].append(
+                    tree([full[half][n, s * 25 + o * 5 + i] * terms[i] for i in range(5)])
                 )
-            ):
-                for j in range(5):
-                    terms = [moved(rows(k, base + 5 * i + j)) for i in range(5)]
-                    at = WIDTH * 8 * k + 8 * (s * 10 + 5 * (n % 2) + j)
-                    for o in range(5):
-                        dest[pl.ds(at + o, 8, stride=WIDTH), :] = tree(
-                            [inverse[o][i] * terms[i] for i in range(5)]
-                        )
-            terms = [moved(upper_rows(k, 50 + i)) for i in range(5)]
-            for o in range(5):
-                totals[o].append(tree([inverse[o][i] * terms[i] for i in range(5)]))
+            yield
         for o in range(5):
-            g[pl.ds(64 * k + o, 8, stride=8), :] = tree(totals[o])
+            g[half][pl.ds(64 * n + o, 8, stride=8), :] = tree(totals[o])
         vv[pl.ds(pl.multiple_of(8 * k, 8), 8), :] = upper_rows(k, 55)
 
-    invert(0, 0)
-
-    def prepare(k, carry):
-        couple(k - 1, (k - 1) % 2)
-        invert(k, k % 2)
-        return carry
-
-    lax.fori_loop(1, 12, prepare, 0)
-    couple(11, 1)
-
-    def product(ref, d, f, step):
+    def product(ref, start, f, step):
         terms = []
-        start = WIDTH * d
         for s in range(4):
             by_y = f if s == 0 else pltpu.roll(f, 32 * s, 1)
             by_z = pltpu.roll(f, (32 * s + step) % 128, 1)
@@ -229,46 +269,89 @@
 
     nothing = jnp.zeros((8, 128), F32)
 
-    def forward_first(d, f):
-        f = jnp.where(inside(d), g[tile(d), :] - product(al, d, f, 1), 0.0)
+    def finish(work):
+        for _ in work:
+            pass
+
+    def sweep(n, half, f, step, update, work=(), share=0):
+        work = iter(work)
+        for m in range(8):
+            e = m if step == 1 else 7 - m
+            d = 16 * n + 8 * half + e
+            matrix = (al if step == 1 else au)[half]
+            coupled = product(matrix, WIDTH * (8 * n + e), f, step)
+            f = update(n, half, e, d, coupled)
+            for _ in range(share):
+                next(work, None)
+        finish(work)
+        return f
+
+    def forward_first(n, half, e, d, coupled):
+        f = jnp.where(inside(d), g[half][pl.ds(64 * n + 8 * e, 8), :] - coupled, 0.0)
         f1[d] = f
         return f
 
-    lax.fori_loop(0, DIAGS, forward_first, nothing)
-
-    def backward_first(n, f):
-        d = DIAGS - 1 - n
-        coupled = product(au, d, f, -1)
+    def backward_first(n, half, e, d, coupled):
         f = jnp.where(inside(d), f1[d] - coupled, 0.0)
         f1[d] = f
-        g[tile(d), :] = coupled
+        h[tile(d), :] = coupled
         return f
 
-    lax.fori_loop(0, DIAGS, backward_first, nothing)
-
-    def forward_second(d, f):
-        coupled = product(al, d, f, 1)
-        f = jnp.where(inside(d), -(g[tile(d), :] + coupled), 0.0)
+    def forward_second(n, half, e, d, coupled):
+        f = jnp.where(inside(d), -(h[tile(d), :] + coupled), 0.0)
         c1[d] = coupled
         return f
 
-    lax.fori_loop(0, DIAGS, forward_second, nothing)
-
-    def backward_second(n, f):
-        d = DIAGS - 1 - n
-        coupled = product(au, d, f, -1)
+    def backward_second(n, half, e, d, coupled):
         f = jnp.where(inside(d), -(c1[d] + coupled), 0.0)
         f1[d] = f1[d] + f
         change[tile(d + 1), :] = jnp.where(inside(d), coupled, 0.0)
         return f
 
+    finish(invert(0, 0))
+    finish(couple_lower(0, 0))
+    finish(start_values(0, 0))
+    finish(invert(0, 1))
+
+    def first_rows(n, f):
+        f = sweep(
+            n, 0, f, 1, forward_first,
+            chain(mixed(couple_lower(n, 1), invert(n + 1, 0)), start_values(n, 1)), SHARE,
+        )
+        return sweep(
+            n, 1, f, 1, forward_first,
+            chain(mixed(couple_lower(n + 1, 0), invert(n + 1, 1)), start_values(n + 1, 0)), SHARE,
+        )
+
+    f = lax.fori_loop(0, 5, first_rows, nothing)
+    f = sweep(5, 0, f, 1, forward_first, chain(couple_lower(5, 1), start_values(5, 1)), 6)
+    sweep(5, 1, f, 1, forward_first, couple_upper(5, 1), 6)
+
+    def last_rows(m, f):
+        n = 5 - m
+        f = sweep(n, 1, f, -1, backward_first, couple_upper(n, 0), 6)
+        return sweep(n, 0, f, -1, backward_first, couple_upper(n - 1, 1), 6)
+
+    f = lax.fori_loop(0, 5, last_rows, nothing)
+    f = sweep(0, 1, f, -1, backward_first, couple_upper(0, 0), 6)
+    sweep(0, 0, f, -1, backward_first)
+
+    def again_forward(n, f):
+        return sweep(n, 1, sweep(n, 0, f, 1, forward_second), 1, forward_second)
+
+    lax.fori_loop(0, 6, again_forward, nothing)
     change[0:8, :] = nothing
-    lax.fori_loop(0, DIAGS, backward_second, nothing)
+
+    def again_backward(m, f):
+        n = 5 - m
+        return sweep(n, 0, sweep(n, 1, f, -1, backward_second), -1, backward_second)
+
+    lax.fori_loop(0, 6, again_backward, nothing)
 
     def residual(d, carry):
         before = change[tile(d), :]
         by_z = pltpu.roll(before, 1, 1)
-        g[tile(d), :] = vv[pl.ds(d, 1), :] * tree(
+        h[tile(d), :] = vv[pl.ds(d, 1), :] * tree(
             [column(tf, d, 75, i) * spread(before, i) for i in range(5)]
             + [column(tf, d, 100, i) * spread(by_z, i) for i in range(5)]
         )
@@ -280,7 +363,7 @@
         for d in range(length):
             f1[d] = jnp.where(far, f1[d + bit], f1[d])
             here, there = pl.ds(8 * d, 8), pl.ds(8 * (d + bit), 8)
-            g[here, :] = jnp.where(far, g[there, :], g[here, :])
+            h[here, :] = jnp.where(far, h[there, :], h[here, :])
 
     owner_y = lane & 15
     owner_z = lane >> 4
@@ -290,7 +373,7 @@
         for jy in range(2):
             y = 4 * n + 2 * side + jy
             value = f1[y]
-            total = g[tile(y), :]
+            total = h[tile(y), :]
             for by in (16, 8, 4, 2, 1):
                 total = total + pltpu.roll(total, 128 - by, 1)
             for jz in range(2):
@@ -334,10 +417,20 @@
     packed = pl.pallas_call(
         pack_kernel,
         out_shape=jax.ShapeDtypeStruct((128 * 24, 128), F32),
-        in_specs=[smem, smem] + [vmem] * 7,
+        in_specs=[smem, smem] + [hbm] * 7,
         out_specs=vmem,
-        scratch_shapes=[pltpu.VMEM((2, 128, 128), F32)],
-        compiler_params=pltpu.CompilerParams(vmem_limit_bytes=32 << 20),
+        scratch_shapes=[
+            pltpu.VMEM((80, 128), F32),
+            pltpu.VMEM((16, 128), jnp.int32),
+            pltpu.VMEM((400, 128), F32),
+            pltpu.VMEM((150, 2, 128), F32),
+            pltpu.VMEM((150, 2, 128), F32),
+            pltpu.VMEM((800, 128), F32),
+            pltpu.VMEM((800, 128), F32),
+            pltpu.VMEM((2, 128, 128), F32),
+            pltpu.SemaphoreType.DMA((7,)),
+        ],
+        compiler_params=pltpu.CompilerParams(vmem_limit_bytes=60 << 20),
         name="pack",
     )(
         meta,
@@ -345,8 +438,8 @@
         rhs.reshape(80, 128),
         codes.reshape(16, 128),
         piv.reshape(400, 128),
-        low_x.reshape(300, 128),
-        up_x.reshape(300, 128),
+        low_x.reshape(150, 2, 128),
+        up_x.reshape(150, 2, 128),
         low.reshape(800, 128),
         up.reshape(800, 128),
     )
@@ -367,14 +460,16 @@
             pltpu.VMEM((96 * ROWS, 128), F32),
             pltpu.VMEM((50 * 128, 128), F32),
             pltpu.VMEM((4, 128, 128), F32),
-            pltpu.VMEM((96 * WIDTH, 128), F32),
-            pltpu.VMEM((96 * WIDTH, 128), F32),
+            *[pltpu.VMEM((48 * WIDTH, 128), F32)] * 4,
+            pltpu.VMEM((48 * 8, 128), F32),
+            pltpu.VMEM((48 * 8, 128), F32),
             pltpu.VMEM((96 * 8, 128), F32),
             pltpu.VMEM((96, 128), F32),
             diag,
             diag,
             pltpu.VMEM((97 * 8, 128), F32),
-            pltpu.VMEM((2, 100, 8, 128), F32),
+            pltpu.VMEM((6, 100, 8, 128), F32),
+            pltpu.VMEM((6, 100, 8, 128), F32),
             pltpu.SemaphoreType.DMA((12,)),
         ],
         compiler_params=pltpu.CompilerParams(vmem_limit_bytes=60 << 20),

time: 210 us -> 195 us (0.929)
  Pallas kernels: 73.4 us -> 65.3 us
  local copies, waits for them, and re-layouts: 8.41 us -> 1.85 us
    pallas_call x1, Pallas kernels: 70.5 us -> 59.5 us  [on_device(): pl.pallas_call(main_kernel, out_shape=jax.ShapeDtypeStruct((128, 128), F3...]
    unnamed x22 -> x8, local copies, waits for them, and re-layouts: 6.29 us -> 1.18 us
    pallas_call x1, Pallas kernels: 1.25 us -> 4.17 us  [on_device(): pl.pallas_call(pack_kernel, out_shape=jax.ShapeDtypeStruct((128 * 24, 128...]
where the time goes in v3:
time: 195 us
  blocking collectives  83.4 us (43%)
  Pallas kernels  65.3 us (33%)
  waiting for transfers between devices  26.4 us (14%)
  starting transfers between devices  17.2 us (9%)
    pallas_call x1, Pallas kernels, on_device(): pl.pallas_call(main_kernel, out_shape=jax.ShapeDtypeStruct((128, 128), F3...  59.5 us
    all_to_all x1, blocking collectives, on_device(): mine = lax.all_to_all(packed.reshape(128, 24, 128), GROUP, 0, 0, tiled=True)  58.9 us
    all_to_all x1, blocking collectives, on_device(): slots = lax.all_to_all(slots.reshape(128, 1, 128), GROUP, 0, 0, tiled=True)  24.5 us
    ppermute x1, waiting for transfers between devices, on_device(): other_x = lax.ppermute(mine, 'xl', SWAP)  23.6 us
    ppermute x1, starting transfers between devices, on_device(): other_cx = lax.ppermute(other_x, 'c', SWAP)  7.89 us
    ppermute x1, starting transfers between devices, on_device(): other_c = lax.ppermute(mine, 'c', SWAP)  7.08 us
    pallas_call x1, Pallas kernels, on_device(): pl.pallas_call(pack_kernel, out_shape=jax.ShapeDtypeStruct((128 * 24, 128...  4.17 us
  transfers between devices with their start and end apart: 3, of which 2 were waited for; matrix products, arithmetic and copies ran while one was open for 0% of the time, Pallas kernels for 0%

profile of v3, /device:TPU:1, one launch (start us, length us, event | category | flops | bytes accessed | tf_op | source)
XLA Modules:
  0.0 194.8 jit_solution(9804946218972438048)
XLA Ops:
  0.6 0.7 stack.31.meta
  1.3 4.2 %pack.1 = f32[3072,128]{1,0:T(8,128)} custom-call(s32[5]{0:T(128)} %stack.31.meta, f32[2,2]{1,0:T(2,128)} %vol.1, f32[80,128]{1,0:T(8,128)} %bitcast.36, s32[16,128]{1,0:T(8,128)} %bitcast.37, f32[400,128]{1,0:T(8,128)} %bitcast.33, f32[150,2,128]{2,1,0:T(2,128)} %bitcast.34, f32[150,2,128]{2,1,0:T(2,128)} %bitcast.35, f32[800,128]{1,0:T(8,128)} %bitcast.29, ...), custom_call_target="tpu_custom_call" | custom-call | tf_op jit(solution)/shard_map/pack/pallas_call | solution.py:417
  5.5 58.9 %all_to_all.10 = f32[128,24,128]{2,1,0:T(8,128)S(1)} all-to-all(f32[128,24,128]{2,1,0:T(8,128)} %bitcast.24), channel_id=1, replica_groups=mesh['cy'=8,'xh'=2,'xl'=2,'z'=8,'c'=2] {'z','cy','xh'}, dimensions={0} | all-to-all | bytes 3145728 | tf_op jit(solution)/shard_map/all_to_all | solution.py:446
  64.4 0.0 copy-start
  64.4 2.2 %collective-permute-start.1 = (f32[128,24,128]{2,1,0:T(8,128)S(1)}, f32[128,24,128]{2,1,0:T(8,128)S(1)}, u32[]{:S(2)}, u32[]{:S(2)}) collective-permute-start(f32[128,24,128]{2,1,0:T(8,128)S(1)} %all_to_all.10), channel_id=1, source_target_pairs={{0,16},{16,0},{1,17},{17,1},{2,18},{18,2},{3,19},{19,3},{4,20},{20... | collective-permute-start | bytes 4718600 | tf_op jit(solution)/shard_map/ppermute | solution.py:447
  66.6 7.1 %collective-permute-start = (f32[128,24,128]{2,1,0:T(8,128)S(1)}, f32[128,24,128]{2,1,0:T(8,128)S(1)}, u32[]{:S(2)}, u32[]{:S(2)}) collective-permute-start(f32[128,24,128]{2,1,0:T(8,128)S(1)} %all_to_all.10), channel_id=1, source_target_pairs={{0,1},{1,0},{2,3},{3,2},{4,5},{5,4},{6,7},{7,6},{8,9},{9,8},{10,11... | collective-permute-start | bytes 4718600 | tf_op jit(solution)/shard_map/ppermute | solution.py:448
  73.7 23.6 %collective-permute-done.1 = f32[128,24,128]{2,1,0:T(8,128)S(1)} collective-permute-done((f32[128,24,128]{2,1,0:T(8,128)S(1)}, f32[128,24,128]{2,1,0:T(8,128)S(1)}, u32[]{:S(2)}, u32[]{:S(2)}) %collective-permute-start.1) | collective-permute-done | bytes 1572896 | tf_op jit(solution)/shard_map/ppermute | solution.py:447
  97.2 0.0 copy-start.1
  97.2 7.9 %collective-permute-start.2 = (f32[128,24,128]{2,1,0:T(8,128)S(1)}, f32[128,24,128]{2,1,0:T(8,128)S(1)}, u32[]{:S(2)}, u32[]{:S(2)}) collective-permute-start(f32[128,24,128]{2,1,0:T(8,128)S(1)} %collective-permute-done.1), channel_id=1, source_target_pairs={{0,1},{1,0},{2,3},{3,2},{4,5},{5,4},{6,7},{7,6},{8,9},{9,8},{10,11... | collective-permute-start | bytes 4718600 | tf_op jit(solution)/shard_map/ppermute | solution.py:449
  105.1 0.0 collective-permute-done
  105.2 0.0 copy-start.2
  105.2 2.8 %collective-permute-done.2 = f32[128,24,128]{2,1,0:T(8,128)S(1)} collective-permute-done((f32[128,24,128]{2,1,0:T(8,128)S(1)}, f32[128,24,128]{2,1,0:T(8,128)S(1)}, u32[]{:S(2)}, u32[]{:S(2)}) %collective-permute-start.2) | collective-permute-done | bytes 1572896 | tf_op jit(solution)/shard_map/ppermute | solution.py:449
  108.0 0.0 copy-done.2
  108.0 0.0 copy-start.3
  108.0 1.2 copy-done.3
  109.2 0.0 copy-done
  109.2 0.0 copy-done.1
  109.2 59.5 %sweeps.1 = f32[128,128]{1,0:T(8,128)} custom-call(s32[5]{0:T(128)} %stack.31.meta, f32[8,16,24,128]{3,2,1,0:T(8,128)} %bitcast.25, f32[8,16,24,128]{3,2,1,0:T(8,128)} %bitcast.27, f32[8,16,24,128]{3,2,1,0:T(8,128)} %bitcast.26, f32[8,16,24,128]{3,2,1,0:T(8,128)} %bitcast.28), custom_call_target="tpu_custom_call" | custom-call | tf_op jit(solution)/shard_map/sweeps/pallas_call | solution.py:452
  168.7 24.5 %all_to_all.11 = f32[128,1,128]{2,1,0:T(1,128)} all-to-all(f32[128,1,128]{2,1,0:T(1,128)} %bitcast.31), channel_id=1, replica_groups=mesh['cy'=8,'xh'=2,'xl'=2,'z'=8,'c'=2] {'z','cy','xh'}, dimensions={0} | all-to-all | bytes 131072 | tf_op jit(solution)/shard_map/all_to_all | solution.py:478
  193.2 1.6 unpack.1
Async XLA Ops:
  64.4 44.8 %copy-start = (f32[128,24,128]{2,1,0:T(8,128)}, f32[128,24,128]{2,1,0:T(8,128)S(1)}, u32[]{:S(2)}) copy-start(f32[128,24,128]{2,1,0:T(8,128)S(1)} %all_to_all.10) | copy-start | bytes 4718596
  64.4 32.9 %collective-permute-start.1 = (f32[128,24,128]{2,1,0:T(8,128)S(1)}, f32[128,24,128]{2,1,0:T(8,128)S(1)}, u32[]{:S(2)}, u32[]{:S(2)}) collective-permute-start(f32[128,24,128]{2,1,0:T(8,128)S(1)} %all_to_all.10), channel_id=1, source_target_pairs={{0,16},{16,0},{1,17},{17,1},{2,18},{18,2},{3,19},{19,3},{4,20},{20... | collective-permute-start | bytes 4718600 | tf_op jit(solution)/shard_map/ppermute | solution.py:447
  66.6 38.6 %collective-permute-start = (f32[128,24,128]{2,1,0:T(8,128)S(1)}, f32[128,24,128]{2,1,0:T(8,128)S(1)}, u32[]{:S(2)}, u32[]{:S(2)}) collective-permute-start(f32[128,24,128]{2,1,0:T(8,128)S(1)} %all_to_all.10), channel_id=1, source_target_pairs={{0,1},{1,0},{2,3},{3,2},{4,5},{5,4},{6,7},{7,6},{8,9},{9,8},{10,11... | collective-permute-start | bytes 4718600 | tf_op jit(solution)/shard_map/ppermute | solution.py:448
  97.2 11.9 %copy-start.1 = (f32[128,24,128]{2,1,0:T(8,128)}, f32[128,24,128]{2,1,0:T(8,128)S(1)}, u32[]{:S(2)}) copy-start(f32[128,24,128]{2,1,0:T(8,128)S(1)} %collective-permute-done.1) | copy-start | bytes 4718596
  97.2 10.7 %collective-permute-start.2 = (f32[128,24,128]{2,1,0:T(8,128)S(1)}, f32[128,24,128]{2,1,0:T(8,128)S(1)}, u32[]{:S(2)}, u32[]{:S(2)}) collective-permute-start(f32[128,24,128]{2,1,0:T(8,128)S(1)} %collective-permute-done.1), channel_id=1, source_target_pairs={{0,1},{1,0},{2,3},{3,2},{4,5},{5,4},{6,7},{7,6},{8,9},{9,8},{10,11... | collective-permute-start | bytes 4718600 | tf_op jit(solution)/shard_map/ppermute | solution.py:449
  105.2 2.8 %copy-start.2 = (f32[128,24,128]{2,1,0:T(8,128)}, f32[128,24,128]{2,1,0:T(8,128)S(1)}, u32[]{:S(2)}) copy-start(f32[128,24,128]{2,1,0:T(8,128)S(1)} %collective-permute-done) | copy-start | bytes 4718596
  108.0 1.2 copy-start.3

commit v4 on v3

--- a/solution.py
+++ b/solution.py
@@ -36,7 +36,7 @@
 
 
 def pack_kernel(
-    meta, vol, rhs_in, codes_in, piv_in, low_x_in, up_x_in, low_in, up_in, out,
+    vol, rhs_in, codes_in, piv_in, low_x_in, up_x_in, low_in, up_in, out,
     rhs, codes, piv, low_x, up_x, low, up, tile, sem,
 ):
     copies = [
@@ -55,10 +55,9 @@
     ]
     for copy in copies:
         copy.start()
-    for copy in copies:
+    for copy in copies[:4]:
         copy.wait()
-    first_z = meta[2]
-    last_z = meta[3]
+    gz = lax.axis_index("z") * 2 + lax.axis_index("c")
     zero = jnp.zeros((25, 128), F32)
     component = lax.broadcasted_iota(jnp.int32, (5, 128), 0)
     for jz in range(2):
@@ -72,10 +71,12 @@
                 t[75:100, :] = low[pl.ds(at, 25, stride=16), :]
                 along_z = low[pl.ds(400 + at, 25, stride=16), :]
                 if jz == 0:
-                    along_z = jnp.where(first_z == 1, 0.0, along_z)
+                    along_z = jnp.where(gz == 0, 0.0, along_z)
                 t[100:125, :] = along_z
                 t[125:128, :] = zero[:3]
                 out[pl.ds(jz * 8 + jy * 4 + p, 128, stride=24), :] = t[...].T
+    for copy in copies[4:]:
+        copy.wait()
     for jz in range(2):
         for p in range(4):
             t = tile.at[p % 2]
@@ -85,7 +86,7 @@
                 t[base : base + 25, :] = up[pl.ds(at, 25, stride=16), :]
                 along_z = up[pl.ds(400 + at, 25, stride=16), :]
                 if jz == 1:
-                    along_z = jnp.where(last_z == 1, 0.0, along_z)
+                    along_z = jnp.where(gz == 15, 0.0, along_z)
                 t[base + 25 : base + 50, :] = along_z
                 code = jnp.broadcast_to(codes[at : at + 1, :], (5, 128))
                 removed = ((code == 1) & (component >= 1) & (component <= 3)) | (
@@ -125,10 +126,10 @@
 
 
 def main_kernel(
-    meta, q0, q1, q2, q3, out, df, du, tf, tu, tmp, al0, al1, au0, au1, g0, g1, h, vv, f1, c1, change, full0, full1, sem
+    q0, q1, q2, q3, out, df, du, tf, tu, tmp, al0, al1, au0, au1, g0, g1, h, vv, f1, c1, full0, full1, sem
 ):
-    core = meta[0]
-    side = meta[1]
+    core = lax.axis_index("c")
+    side = lax.axis_index("xl")
     copies = []
     for n, (q, dc, dx) in enumerate(((q0, 0, 0), (q1, 1, 0), (q2, 0, 1), (q3, 1, 1))):
         c = core + dc - 2 * core * dc
@@ -139,9 +140,12 @@
                 df.at[:, c, part, pl.ds(0, 16), x] if part < 2 else du.at[:, c, pl.ds(0, 16), x]
             )
             copies.append(pltpu.make_async_copy(src, dst, sem.at[n * 3 + part]))
-    for copy in copies:
+    for copy in copies[2::3]:
         copy.start()
-    for copy in copies:
+    for part in range(2):
+        for copy in copies[part::3]:
+            copy.start()
+    for copy in copies[2::3]:
         copy.wait()
     fl = df.reshape(32 * PITCH, 128)
     ul = du.reshape(16 * PITCH, 128)
@@ -149,15 +153,6 @@
     sub = lax.broadcasted_iota(jnp.int32, (8, 128), 0)
     z = lane & 31
     even_z = (lane & 1) == 0
-
-    def turn_f(d, carry):
-        block = jnp.concatenate(
-            [fl[pl.ds(4 * d + p, 32, stride=PITCH - 4), :] for p in range(4)], axis=0
-        )
-        tf[pl.ds(ROWS * d, 128), :] = block.T
-        return carry
-
-    lax.fori_loop(0, DIAGS, turn_f, 0, unroll=5)
 
     def turn_u(n, carry):
         for k in range(4):
@@ -171,6 +166,19 @@
         return carry
 
     lax.fori_loop(0, 12, turn_u, 0)
+
+    for part in range(2):
+        for copy in copies[part::3]:
+            copy.wait()
+
+    def turn_f(d, carry):
+        block = jnp.concatenate(
+            [fl[pl.ds(4 * d + p, 32, stride=PITCH - 4), :] for p in range(4)], axis=0
+        )
+        tf[pl.ds(ROWS * d, 128), :] = block.T
+        return carry
+
+    lax.fori_loop(0, DIAGS, turn_f, 0, unroll=5)
 
     def lower_rows(k, r):
         return tf[pl.ds(ROWS * 8 * k + r, 8, stride=ROWS), :]
@@ -251,15 +259,22 @@
         vv[pl.ds(pl.multiple_of(8 * k, 8), 8), :] = upper_rows(k, 55)
 
     def product(ref, start, f, step):
-        terms = []
+        sums = []
         for s in range(4):
-            by_y = f if s == 0 else pltpu.roll(f, 32 * s, 1)
-            by_z = pltpu.roll(f, (32 * s + step) % 128, 1)
-            for i in range(5):
-                terms.append(ref[pl.ds(start + 8 * (s * 10 + i), 8), :] * spread(by_y, i))
-            for i in range(5):
-                terms.append(ref[pl.ds(start + 8 * (s * 10 + 5 + i), 8), :] * spread(by_z, i))
-        return tree(terms)
+            for m, by in enumerate((32 * s, (32 * s + step) % 128)):
+                v = f if by == 0 else pltpu.roll(f, by, 1)
+                sums.append(
+                    tree(
+                        [
+                            ref[pl.ds(start + 8 * (s * 10 + 5 * m + i), 8), :] * spread(v, i)
+                            for i in range(5)
+                        ]
+                    )
+                )
+        late = sums[1]
+        for v in sums[2:]:
+            late = late + v
+        return sums[0], late
 
     def tile(d):
         return pl.ds(pl.multiple_of(8 * d, 8), 8)
@@ -279,33 +294,38 @@
             e = m if step == 1 else 7 - m
             d = 16 * n + 8 * half + e
             matrix = (al if step == 1 else au)[half]
-            coupled = product(matrix, WIDTH * (8 * n + e), f, step)
-            f = update(n, half, e, d, coupled)
+            early, late = product(matrix, WIDTH * (8 * n + e), f, step)
+            f = update(n, half, e, d, early, late)
             for _ in range(share):
                 next(work, None)
         finish(work)
         return f
 
-    def forward_first(n, half, e, d, coupled):
-        f = jnp.where(inside(d), g[half][pl.ds(64 * n + 8 * e, 8), :] - coupled, 0.0)
+    def forward_first(n, half, e, d, early, late):
+        f = jnp.where(inside(d), (g[half][pl.ds(64 * n + 8 * e, 8), :] - early) - late, 0.0)
         f1[d] = f
         return f
 
-    def backward_first(n, half, e, d, coupled):
-        f = jnp.where(inside(d), f1[d] - coupled, 0.0)
+    def backward_first(n, half, e, d, early, late):
+        f = jnp.where(inside(d), (f1[d] - early) - late, 0.0)
         f1[d] = f
-        h[tile(d), :] = coupled
+        h[tile(d), :] = early + late
         return f
 
-    def forward_second(n, half, e, d, coupled):
-        f = jnp.where(inside(d), -(h[tile(d), :] + coupled), 0.0)
-        c1[d] = coupled
+    def forward_second(n, half, e, d, early, late):
+        f = jnp.where(inside(d), -(h[tile(d), :] + early) - late, 0.0)
+        c1[d] = early + late
         return f
 
-    def backward_second(n, half, e, d, coupled):
-        f = jnp.where(inside(d), -(c1[d] + coupled), 0.0)
+    def backward_second(n, half, e, d, early, late):
+        f = jnp.where(inside(d), -(c1[d] + early) - late, 0.0)
         f1[d] = f1[d] + f
-        change[tile(d + 1), :] = jnp.where(inside(d), coupled, 0.0)
+        change = jnp.where(inside(d), early + late, 0.0)
+        by_z = pltpu.roll(change, 1, 1)
+        h[tile(d + 1), :] = vv[pl.ds(d + 1, 1), :] * tree(
+            [column(tf, d + 1, 75, i) * spread(change, i) for i in range(5)]
+            + [column(tf, d + 1, 100, i) * spread(by_z, i) for i in range(5)]
+        )
         return f
 
     finish(invert(0, 0))
@@ -340,7 +360,7 @@
         return sweep(n, 1, sweep(n, 0, f, 1, forward_second), 1, forward_second)
 
     lax.fori_loop(0, 6, again_forward, nothing)
-    change[0:8, :] = nothing
+    h[0:8, :] = nothing
 
     def again_backward(m, f):
         n = 5 - m
@@ -348,16 +368,6 @@
 
     lax.fori_loop(0, 6, again_backward, nothing)
 
-    def residual(d, carry):
-        before = change[tile(d), :]
-        by_z = pltpu.roll(before, 1, 1)
-        h[tile(d), :] = vv[pl.ds(d, 1), :] * tree(
-            [column(tf, d, 75, i) * spread(before, i) for i in range(5)]
-            + [column(tf, d, 100, i) * spread(by_z, i) for i in range(5)]
-        )
-        return carry
-
-    lax.fori_loop(0, DIAGS, residual, 0, unroll=5)
     for bit, length in ((16, 79), (8, 71), (4, 67), (2, 65), (1, 64)):
         far = (z & bit) != 0
         for d in range(length):
@@ -389,9 +399,9 @@
     out[...] = jnp.concatenate(slots, axis=0).T
 
 
-def unpack_kernel(meta, slots, correction, coarse):
+def unpack_kernel(slots, correction, coarse):
     values = slots[...].T
-    gz = meta[4]
+    gz = lax.axis_index("z") * 2 + lax.axis_index("c")
     for p in range(4):
         for jy in range(2):
             for jz in range(2):
@@ -405,19 +415,13 @@
 
 
 def on_device(rhs, codes, piv, low_x, up_x, low, up, volume):
-    core = lax.axis_index("c")
-    side = lax.axis_index("xl")
-    gz = lax.axis_index("z") * 2 + core
-    meta = jnp.stack(
-        [core, side, (gz == 0).astype(jnp.int32), (gz == 15).astype(jnp.int32), gz]
-    ).astype(jnp.int32)
     smem = pl.BlockSpec(memory_space=SMEM)
     vmem = pl.BlockSpec(memory_space=VMEM)
     hbm = pl.BlockSpec(memory_space=pl.ANY)
     packed = pl.pallas_call(
         pack_kernel,
         out_shape=jax.ShapeDtypeStruct((128 * 24, 128), F32),
-        in_specs=[smem, smem] + [hbm] * 7,
+        in_specs=[smem] + [hbm] * 7,
         out_specs=vmem,
         scratch_shapes=[
             pltpu.VMEM((80, 128), F32),
@@ -433,7 +437,6 @@
         compiler_params=pltpu.CompilerParams(vmem_limit_bytes=60 << 20),
         name="pack",
     )(
-        meta,
         volume,
         rhs.reshape(80, 128),
         codes.reshape(16, 128),
@@ -452,29 +455,28 @@
     slots = pl.pallas_call(
         main_kernel,
         out_shape=jax.ShapeDtypeStruct((128, 128), F32),
-        in_specs=[smem] + [hbm] * 4,
+        in_specs=[hbm] * 4,
         out_specs=vmem,
         scratch_shapes=[
             pltpu.VMEM((8, 2, 2, 17, 2, 8, 128), F32),
             pltpu.VMEM((8, 2, 17, 2, 8, 128), F32),
-            pltpu.VMEM((96 * ROWS, 128), F32),
+            pltpu.VMEM((98 * ROWS, 128), F32),
             pltpu.VMEM((50 * 128, 128), F32),
             pltpu.VMEM((4, 128, 128), F32),
             *[pltpu.VMEM((48 * WIDTH, 128), F32)] * 4,
             pltpu.VMEM((48 * 8, 128), F32),
             pltpu.VMEM((48 * 8, 128), F32),
-            pltpu.VMEM((96 * 8, 128), F32),
-            pltpu.VMEM((96, 128), F32),
+            pltpu.VMEM((97 * 8, 128), F32),
+            pltpu.VMEM((104, 128), F32),
             diag,
             diag,
-            pltpu.VMEM((97 * 8, 128), F32),
             pltpu.VMEM((6, 100, 8, 128), F32),
             pltpu.VMEM((6, 100, 8, 128), F32),
             pltpu.SemaphoreType.DMA((12,)),
         ],
         compiler_params=pltpu.CompilerParams(vmem_limit_bytes=60 << 20),
         name="sweeps",
-    )(meta, *quarters)
+    )(*quarters)
     slots = lax.all_to_all(slots.reshape(128, 1, 128), GROUP, 0, 0, tiled=True)
     correction, coarse = pl.pallas_call(
         unpack_kernel,
@@ -482,10 +484,10 @@
             jax.ShapeDtypeStruct((80, 128), F32),
             jax.ShapeDtypeStruct((40, 128), F32),
         ),
-        in_specs=[smem, vmem],
+        in_specs=[vmem],
         out_specs=(vmem, vmem),
         name="unpack",
-    )(meta, slots.reshape(128, 128))
+    )(slots.reshape(128, 128))
     return correction.reshape(5, 4, 2, 2, 128), coarse[:, :8].reshape(5, 4, 2, 8)
 
 

time: 195 us -> 192 us (0.985)
  Pallas kernels: 65.3 us -> 63 us
    pallas_call x1, Pallas kernels: 59.5 us -> 57.3 us  [on_device(): pl.pallas_call(main_kernel, out_shape=jax.ShapeDtypeStruct((128, 128), F3...]
where the time goes in v4:
time: 192 us
  blocking collectives  83.4 us (43%)
  Pallas kernels  63 us (33%)
  waiting for transfers between devices  26.4 us (14%)
  starting transfers between devices  17.2 us (9%)
    all_to_all x1, blocking collectives, on_device(): mine = lax.all_to_all(packed.reshape(128, 24, 128), GROUP, 0, 0, tiled=True)  58.9 us
    pallas_call x1, Pallas kernels, on_device(): pl.pallas_call(main_kernel, out_shape=jax.ShapeDtypeStruct((128, 128), F3...  57.3 us
    all_to_all x1, blocking collectives, on_device(): slots = lax.all_to_all(slots.reshape(128, 1, 128), GROUP, 0, 0, tiled=True)  24.5 us
    ppermute x1, waiting for transfers between devices, on_device(): other_x = lax.ppermute(mine, 'xl', SWAP)  23.6 us
    ppermute x1, starting transfers between devices, on_device(): other_cx = lax.ppermute(other_x, 'c', SWAP)  7.89 us
    ppermute x1, starting transfers between devices, on_device(): other_c = lax.ppermute(mine, 'c', SWAP)  7.08 us
    pallas_call x1, Pallas kernels, on_device(): pl.pallas_call(pack_kernel, out_shape=jax.ShapeDtypeStruct((128 * 24, 128...  4.1 us
  transfers between devices with their start and end apart: 3, of which 2 were waited for; matrix products, arithmetic and copies ran while one was open for 0% of the time, Pallas kernels for 0%

profile of v4, /device:TPU:1, one launch (start us, length us, event | category | flops | bytes accessed | tf_op | source)
XLA Modules:
  0.0 191.8 jit_solution(9156830545486157673)
XLA Ops:
  0.6 4.1 %pack.1 = f32[3072,128]{1,0:T(8,128)} custom-call(f32[2,2]{1,0:T(2,128)} %vol.1, f32[80,128]{1,0:T(8,128)} %bitcast.31, s32[16,128]{1,0:T(8,128)} %bitcast.32, f32[400,128]{1,0:T(8,128)} %bitcast.28, f32[150,2,128]{2,1,0:T(2,128)} %bitcast.29, f32[150,2,128]{2,1,0:T(2,128)} %bitcast.30, f32[800,128]{1,0:T(8,128)} %bitcast.24, f32[800,128]{1,0:T(8,128)} %bitcast.25), custom_call_target="tpu_custom_call" | custom-call | tf_op jit(solution)/shard_map/pack/pallas_call | solution.py:421
  4.7 58.9 %all_to_all.10 = f32[128,24,128]{2,1,0:T(8,128)S(1)} all-to-all(f32[128,24,128]{2,1,0:T(8,128)} %bitcast.20), channel_id=1, replica_groups=mesh['cy'=8,'xh'=2,'xl'=2,'z'=8,'c'=2] {'z','cy','xh'}, dimensions={0} | all-to-all | bytes 3145728 | tf_op jit(solution)/shard_map/all_to_all | solution.py:449
  63.6 0.0 copy-start
  63.6 2.2 %collective-permute-start.1 = (f32[128,24,128]{2,1,0:T(8,128)S(1)}, f32[128,24,128]{2,1,0:T(8,128)S(1)}, u32[]{:S(2)}, u32[]{:S(2)}) collective-permute-start(f32[128,24,128]{2,1,0:T(8,128)S(1)} %all_to_all.10), channel_id=1, source_target_pairs={{0,16},{16,0},{1,17},{17,1},{2,18},{18,2},{3,19},{19,3},{4,20},{20... | collective-permute-start | bytes 4718600 | tf_op jit(solution)/shard_map/ppermute | solution.py:450
  65.8 7.1 %collective-permute-start = (f32[128,24,128]{2,1,0:T(8,128)S(1)}, f32[128,24,128]{2,1,0:T(8,128)S(1)}, u32[]{:S(2)}, u32[]{:S(2)}) collective-permute-start(f32[128,24,128]{2,1,0:T(8,128)S(1)} %all_to_all.10), channel_id=1, source_target_pairs={{0,1},{1,0},{2,3},{3,2},{4,5},{5,4},{6,7},{7,6},{8,9},{9,8},{10,11... | collective-permute-start | bytes 4718600 | tf_op jit(solution)/shard_map/ppermute | solution.py:451
  72.9 23.6 %collective-permute-done.1 = f32[128,24,128]{2,1,0:T(8,128)S(1)} collective-permute-done((f32[128,24,128]{2,1,0:T(8,128)S(1)}, f32[128,24,128]{2,1,0:T(8,128)S(1)}, u32[]{:S(2)}, u32[]{:S(2)}) %collective-permute-start.1) | collective-permute-done | bytes 1572896 | tf_op jit(solution)/shard_map/ppermute | solution.py:450
  96.5 0.0 copy-start.1
  96.5 7.9 %collective-permute-start.2 = (f32[128,24,128]{2,1,0:T(8,128)S(1)}, f32[128,24,128]{2,1,0:T(8,128)S(1)}, u32[]{:S(2)}, u32[]{:S(2)}) collective-permute-start(f32[128,24,128]{2,1,0:T(8,128)S(1)} %collective-permute-done.1), channel_id=1, source_target_pairs={{0,1},{1,0},{2,3},{3,2},{4,5},{5,4},{6,7},{7,6},{8,9},{9,8},{10,11... | collective-permute-start | bytes 4718600 | tf_op jit(solution)/shard_map/ppermute | solution.py:452
  104.4 0.0 collective-permute-done
  104.4 0.0 copy-start.2
  104.4 2.8 %collective-permute-done.2 = f32[128,24,128]{2,1,0:T(8,128)S(1)} collective-permute-done((f32[128,24,128]{2,1,0:T(8,128)S(1)}, f32[128,24,128]{2,1,0:T(8,128)S(1)}, u32[]{:S(2)}, u32[]{:S(2)}) %collective-permute-start.2) | collective-permute-done | bytes 1572896 | tf_op jit(solution)/shard_map/ppermute | solution.py:452
  107.2 0.0 copy-done.2
  107.2 0.0 copy-start.3
  107.2 1.2 copy-done.3
  108.4 0.0 copy-done
  108.4 0.0 copy-done.1
  108.4 57.3 %sweeps.1 = f32[128,128]{1,0:T(8,128)} custom-call(f32[8,16,24,128]{3,2,1,0:T(8,128)} %bitcast.19, f32[8,16,24,128]{3,2,1,0:T(8,128)} %bitcast.22, f32[8,16,24,128]{3,2,1,0:T(8,128)} %bitcast.21, f32[8,16,24,128]{3,2,1,0:T(8,128)} %bitcast.23), custom_call_target="tpu_custom_call" | custom-call | tf_op jit(solution)/shard_map/sweeps/pallas_call | solution.py:455
  165.7 24.5 %all_to_all.11 = f32[128,1,128]{2,1,0:T(1,128)} all-to-all(f32[128,1,128]{2,1,0:T(1,128)} %bitcast.26), channel_id=1, replica_groups=mesh['cy'=8,'xh'=2,'xl'=2,'z'=8,'c'=2] {'z','cy','xh'}, dimensions={0} | all-to-all | bytes 131072 | tf_op jit(solution)/shard_map/all_to_all | solution.py:480
  190.2 1.6 unpack.1
Async XLA Ops:
  63.6 44.8 %copy-start = (f32[128,24,128]{2,1,0:T(8,128)}, f32[128,24,128]{2,1,0:T(8,128)S(1)}, u32[]{:S(2)}) copy-start(f32[128,24,128]{2,1,0:T(8,128)S(1)} %all_to_all.10) | copy-start | bytes 4718596
  63.6 32.9 %collective-permute-start.1 = (f32[128,24,128]{2,1,0:T(8,128)S(1)}, f32[128,24,128]{2,1,0:T(8,128)S(1)}, u32[]{:S(2)}, u32[]{:S(2)}) collective-permute-start(f32[128,24,128]{2,1,0:T(8,128)S(1)} %all_to_all.10), channel_id=1, source_target_pairs={{0,16},{16,0},{1,17},{17,1},{2,18},{18,2},{3,19},{19,3},{4,20},{20... | collective-permute-start | bytes 4718600 | tf_op jit(solution)/shard_map/ppermute | solution.py:450
  65.8 38.6 %collective-permute-start = (f32[128,24,128]{2,1,0:T(8,128)S(1)}, f32[128,24,128]{2,1,0:T(8,128)S(1)}, u32[]{:S(2)}, u32[]{:S(2)}) collective-permute-start(f32[128,24,128]{2,1,0:T(8,128)S(1)} %all_to_all.10), channel_id=1, source_target_pairs={{0,1},{1,0},{2,3},{3,2},{4,5},{5,4},{6,7},{7,6},{8,9},{9,8},{10,11... | collective-permute-start | bytes 4718600 | tf_op jit(solution)/shard_map/ppermute | solution.py:451
  96.5 11.9 %copy-start.1 = (f32[128,24,128]{2,1,0:T(8,128)}, f32[128,24,128]{2,1,0:T(8,128)S(1)}, u32[]{:S(2)}) copy-start(f32[128,24,128]{2,1,0:T(8,128)S(1)} %collective-permute-done.1) | copy-start | bytes 4718596
  96.5 10.7 %collective-permute-start.2 = (f32[128,24,128]{2,1,0:T(8,128)S(1)}, f32[128,24,128]{2,1,0:T(8,128)S(1)}, u32[]{:S(2)}, u32[]{:S(2)}) collective-permute-start(f32[128,24,128]{2,1,0:T(8,128)S(1)} %collective-permute-done.1), channel_id=1, source_target_pairs={{0,1},{1,0},{2,3},{3,2},{4,5},{5,4},{6,7},{7,6},{8,9},{9,8},{10,11... | collective-permute-start | bytes 4718600 | tf_op jit(solution)/shard_map/ppermute | solution.py:452
  104.4 2.8 %copy-start.2 = (f32[128,24,128]{2,1,0:T(8,128)}, f32[128,24,128]{2,1,0:T(8,128)S(1)}, u32[]{:S(2)}) copy-start(f32[128,24,128]{2,1,0:T(8,128)S(1)} %collective-permute-done) | copy-start | bytes 4718596
  107.2 1.2 copy-start.3

commit v5 on v4

--- a/solution.py
+++ b/solution.py
@@ -64,7 +64,7 @@
         for jy in range(2):
             for p in range(4):
                 at = p * 4 + jy * 2 + jz
-                t = tile.at[(jy * 4 + p) % 2]
+                t = tile.at[jy * 4 + p]
                 t[0:25, :] = piv[pl.ds(at, 25, stride=16), :]
                 t[25:50, :] = low_x[pl.ds(2 * p - 2 + jy, 25, stride=6), jz, :] if p > 0 else zero
                 t[50:75, :] = up_x[pl.ds(2 * p + jy, 25, stride=6), jz, :] if p < 3 else zero
@@ -79,7 +79,7 @@
         copy.wait()
     for jz in range(2):
         for p in range(4):
-            t = tile.at[p % 2]
+            t = tile.at[jz * 4 + p]
             for jy in range(2):
                 at = p * 4 + jy * 2 + jz
                 base = 64 * jy
@@ -155,8 +155,8 @@
     even_z = (lane & 1) == 0
 
     def turn_u(n, carry):
-        for k in range(4):
-            e = 4 * n + k
+        for k in range(8):
+            e = 8 * n + k
             for p in range(4):
                 for jz in range(2):
                     tmp[k, pl.ds(p * 32 + jz, 16, stride=2), :] = ul[
@@ -165,7 +165,7 @@
             tu[pl.ds(pl.multiple_of(128 * e + 128, 128), 128), :] = tmp[k].T
         return carry
 
-    lax.fori_loop(0, 12, turn_u, 0)
+    lax.fori_loop(0, 6, turn_u, 0)
 
     for part in range(2):
         for copy in copies[part::3]:
@@ -178,7 +178,7 @@
         tf[pl.ds(ROWS * d, 128), :] = block.T
         return carry
 
-    lax.fori_loop(0, DIAGS, turn_f, 0, unroll=5)
+    lax.fori_loop(0, DIAGS, turn_f, 0, unroll=19)
 
     def lower_rows(k, r):
         return tf[pl.ds(ROWS * 8 * k + r, 8, stride=ROWS), :]
@@ -271,10 +271,7 @@
                         ]
                     )
                 )
-        late = sums[1]
-        for v in sums[2:]:
-            late = late + v
-        return sums[0], late
+        return sums[0], tree(sums[1:])
 
     def tile(d):
         return pl.ds(pl.multiple_of(8 * d, 8), 8)
@@ -395,7 +392,7 @@
                     sums[k] = jnp.where(owner_y == n, picked, sums[k])
         return tuple(sums)
 
-    slots = lax.fori_loop(0, 16, collect, (nothing,) * 16, unroll=4)
+    slots = lax.fori_loop(0, 16, collect, (nothing,) * 16, unroll=8)
     out[...] = jnp.concatenate(slots, axis=0).T
 
 
@@ -431,7 +428,7 @@
             pltpu.VMEM((150, 2, 128), F32),
             pltpu.VMEM((800, 128), F32),
             pltpu.VMEM((800, 128), F32),
-            pltpu.VMEM((2, 128, 128), F32),
+            pltpu.VMEM((8, 128, 128), F32),
             pltpu.SemaphoreType.DMA((7,)),
         ],
         compiler_params=pltpu.CompilerParams(vmem_limit_bytes=60 << 20),
@@ -462,7 +459,7 @@
             pltpu.VMEM((8, 2, 17, 2, 8, 128), F32),
             pltpu.VMEM((98 * ROWS, 128), F32),
             pltpu.VMEM((50 * 128, 128), F32),
-            pltpu.VMEM((4, 128, 128), F32),
+            pltpu.VMEM((8, 128, 128), F32),
             *[pltpu.VMEM((48 * WIDTH, 128), F32)] * 4,
             pltpu.VMEM((48 * 8, 128), F32),
             pltpu.VMEM((48 * 8, 128), F32),

time: 192 us -> 190 us (0.990)
  Pallas kernels: 63 us -> 60.6 us
    pallas_call x1, Pallas kernels: 57.3 us -> 54.9 us  [on_device(): pl.pallas_call(main_kernel, out_shape=jax.ShapeDtypeStruct((128, 128), F3...]
where the time goes in v5:
time: 190 us; the launch traced here: 189 us
  blocking collectives  83.4 us (44%)
  Pallas kernels  60.6 us (32%)
  waiting for transfers between devices  26.4 us (14%)
  starting transfers between devices  17.2 us (9%)
    all_to_all x1, blocking collectives, on_device(): mine = lax.all_to_all(packed.reshape(128, 24, 128), GROUP, 0, 0, tiled=True)  58.9 us
    pallas_call x1, Pallas kernels, on_device(): pl.pallas_call(main_kernel, out_shape=jax.ShapeDtypeStruct((128, 128), F3...  54.9 us
    all_to_all x1, blocking collectives, on_device(): slots = lax.all_to_all(slots.reshape(128, 1, 128), GROUP, 0, 0, tiled=True)  24.5 us
    ppermute x1, waiting for transfers between devices, on_device(): other_x = lax.ppermute(mine, 'xl', SWAP)  23.6 us
    ppermute x1, starting transfers between devices, on_device(): other_cx = lax.ppermute(other_x, 'c', SWAP)  7.89 us
    ppermute x1, starting transfers between devices, on_device(): other_c = lax.ppermute(mine, 'c', SWAP)  7.08 us
    pallas_call x1, Pallas kernels, on_device(): pl.pallas_call(pack_kernel, out_shape=jax.ShapeDtypeStruct((128 * 24, 128...  4.16 us
  transfers between devices with their start and end apart: 3, of which 2 were waited for; matrix products, arithmetic and copies ran while one was open for 0% of the time, Pallas kernels for 0%

profile of v5, /device:TPU:1, one launch (start us, length us, event | category | flops | bytes accessed | tf_op | source)
XLA Modules:
  0.0 189.5 jit_solution(9848848218233370204)
XLA Ops:
  0.6 4.2 %pack.1 = f32[3072,128]{1,0:T(8,128)} custom-call(f32[2,2]{1,0:T(2,128)} %vol.1, f32[80,128]{1,0:T(8,128)} %bitcast.31, s32[16,128]{1,0:T(8,128)} %bitcast.32, f32[400,128]{1,0:T(8,128)} %bitcast.28, f32[150,2,128]{2,1,0:T(2,128)} %bitcast.29, f32[150,2,128]{2,1,0:T(2,128)} %bitcast.30, f32[800,128]{1,0:T(8,128)} %bitcast.24, f32[800,128]{1,0:T(8,128)} %bitcast.25), custom_call_target="tpu_custom_call" | custom-call | tf_op jit(solution)/shard_map/pack/pallas_call | solution.py:418
  4.8 58.9 %all_to_all.10 = f32[128,24,128]{2,1,0:T(8,128)S(1)} all-to-all(f32[128,24,128]{2,1,0:T(8,128)} %bitcast.20), channel_id=1, replica_groups=mesh['cy'=8,'xh'=2,'xl'=2,'z'=8,'c'=2] {'z','cy','xh'}, dimensions={0} | all-to-all | bytes 3145728 | tf_op jit(solution)/shard_map/all_to_all | solution.py:446
  63.7 0.0 copy-start
  63.7 2.2 %collective-permute-start.1 = (f32[128,24,128]{2,1,0:T(8,128)S(1)}, f32[128,24,128]{2,1,0:T(8,128)S(1)}, u32[]{:S(2)}, u32[]{:S(2)}) collective-permute-start(f32[128,24,128]{2,1,0:T(8,128)S(1)} %all_to_all.10), channel_id=1, source_target_pairs={{0,16},{16,0},{1,17},{17,1},{2,18},{18,2},{3,19},{19,3},{4,20},{20... | collective-permute-start | bytes 4718600 | tf_op jit(solution)/shard_map/ppermute | solution.py:447
  65.9 7.1 %collective-permute-start = (f32[128,24,128]{2,1,0:T(8,128)S(1)}, f32[128,24,128]{2,1,0:T(8,128)S(1)}, u32[]{:S(2)}, u32[]{:S(2)}) collective-permute-start(f32[128,24,128]{2,1,0:T(8,128)S(1)} %all_to_all.10), channel_id=1, source_target_pairs={{0,1},{1,0},{2,3},{3,2},{4,5},{5,4},{6,7},{7,6},{8,9},{9,8},{10,11... | collective-permute-start | bytes 4718600 | tf_op jit(solution)/shard_map/ppermute | solution.py:448
  73.0 23.6 %collective-permute-done.1 = f32[128,24,128]{2,1,0:T(8,128)S(1)} collective-permute-done((f32[128,24,128]{2,1,0:T(8,128)S(1)}, f32[128,24,128]{2,1,0:T(8,128)S(1)}, u32[]{:S(2)}, u32[]{:S(2)}) %collective-permute-start.1) | collective-permute-done | bytes 1572896 | tf_op jit(solution)/shard_map/ppermute | solution.py:447
  96.6 0.0 copy-start.1
  96.6 7.9 %collective-permute-start.2 = (f32[128,24,128]{2,1,0:T(8,128)S(1)}, f32[128,24,128]{2,1,0:T(8,128)S(1)}, u32[]{:S(2)}, u32[]{:S(2)}) collective-permute-start(f32[128,24,128]{2,1,0:T(8,128)S(1)} %collective-permute-done.1), channel_id=1, source_target_pairs={{0,1},{1,0},{2,3},{3,2},{4,5},{5,4},{6,7},{7,6},{8,9},{9,8},{10,11... | collective-permute-start | bytes 4718600 | tf_op jit(solution)/shard_map/ppermute | solution.py:449
  104.5 0.0 collective-permute-done
  104.5 0.0 copy-start.2
  104.5 2.8 %collective-permute-done.2 = f32[128,24,128]{2,1,0:T(8,128)S(1)} collective-permute-done((f32[128,24,128]{2,1,0:T(8,128)S(1)}, f32[128,24,128]{2,1,0:T(8,128)S(1)}, u32[]{:S(2)}, u32[]{:S(2)}) %collective-permute-start.2) | collective-permute-done | bytes 1572896 | tf_op jit(solution)/shard_map/ppermute | solution.py:449
  107.3 0.0 copy-done.2
  107.3 0.0 copy-start.3
  107.3 1.2 copy-done.3
  108.5 0.0 copy-done
  108.5 0.0 copy-done.1
  108.5 54.9 %sweeps.1 = f32[128,128]{1,0:T(8,128)} custom-call(f32[8,16,24,128]{3,2,1,0:T(8,128)} %bitcast.19, f32[8,16,24,128]{3,2,1,0:T(8,128)} %bitcast.22, f32[8,16,24,128]{3,2,1,0:T(8,128)} %bitcast.21, f32[8,16,24,128]{3,2,1,0:T(8,128)} %bitcast.23), custom_call_target="tpu_custom_call" | custom-call | tf_op jit(solution)/shard_map/sweeps/pallas_call | solution.py:452
  163.4 24.5 %all_to_all.11 = f32[128,1,128]{2,1,0:T(1,128)} all-to-all(f32[128,1,128]{2,1,0:T(1,128)} %bitcast.26), channel_id=1, replica_groups=mesh['cy'=8,'xh'=2,'xl'=2,'z'=8,'c'=2] {'z','cy','xh'}, dimensions={0} | all-to-all | bytes 131072 | tf_op jit(solution)/shard_map/all_to_all | solution.py:477
  187.8 1.6 unpack.1
Async XLA Ops:
  63.7 44.8 %copy-start = (f32[128,24,128]{2,1,0:T(8,128)}, f32[128,24,128]{2,1,0:T(8,128)S(1)}, u32[]{:S(2)}) copy-start(f32[128,24,128]{2,1,0:T(8,128)S(1)} %all_to_all.10) | copy-start | bytes 4718596
  63.7 32.9 %collective-permute-start.1 = (f32[128,24,128]{2,1,0:T(8,128)S(1)}, f32[128,24,128]{2,1,0:T(8,128)S(1)}, u32[]{:S(2)}, u32[]{:S(2)}) collective-permute-start(f32[128,24,128]{2,1,0:T(8,128)S(1)} %all_to_all.10), channel_id=1, source_target_pairs={{0,16},{16,0},{1,17},{17,1},{2,18},{18,2},{3,19},{19,3},{4,20},{20... | collective-permute-start | bytes 4718600 | tf_op jit(solution)/shard_map/ppermute | solution.py:447
  65.9 38.6 %collective-permute-start = (f32[128,24,128]{2,1,0:T(8,128)S(1)}, f32[128,24,128]{2,1,0:T(8,128)S(1)}, u32[]{:S(2)}, u32[]{:S(2)}) collective-permute-start(f32[128,24,128]{2,1,0:T(8,128)S(1)} %all_to_all.10), channel_id=1, source_target_pairs={{0,1},{1,0},{2,3},{3,2},{4,5},{5,4},{6,7},{7,6},{8,9},{9,8},{10,11... | collective-permute-start | bytes 4718600 | tf_op jit(solution)/shard_map/ppermute | solution.py:448
  96.6 11.9 %copy-start.1 = (f32[128,24,128]{2,1,0:T(8,128)}, f32[128,24,128]{2,1,0:T(8,128)S(1)}, u32[]{:S(2)}) copy-start(f32[128,24,128]{2,1,0:T(8,128)S(1)} %collective-permute-done.1) | copy-start | bytes 4718596
  96.6 10.7 %collective-permute-start.2 = (f32[128,24,128]{2,1,0:T(8,128)S(1)}, f32[128,24,128]{2,1,0:T(8,128)S(1)}, u32[]{:S(2)}, u32[]{:S(2)}) collective-permute-start(f32[128,24,128]{2,1,0:T(8,128)S(1)} %collective-permute-done.1), channel_id=1, source_target_pairs={{0,1},{1,0},{2,3},{3,2},{4,5},{5,4},{6,7},{7,6},{8,9},{9,8},{10,11... | collective-permute-start | bytes 4718600 | tf_op jit(solution)/shard_map/ppermute | solution.py:449
  104.5 2.8 %copy-start.2 = (f32[128,24,128]{2,1,0:T(8,128)}, f32[128,24,128]{2,1,0:T(8,128)S(1)}, u32[]{:S(2)}) copy-start(f32[128,24,128]{2,1,0:T(8,128)S(1)} %collective-permute-done) | copy-start | bytes 4718596
  107.3 1.2 copy-start.3
